TPU v7x, 512 devices: a whole 4x4x16 slice. The times are simulated.
512 devices in a mesh: wide: 64 (over y, z), narrow: 8 (over x, core).
Axes of the slice: x: 4, y: 4, z: 16, core: 2. Of those that a mesh axis runs over, the one named last changes fastest.
Arguments:
- coefficients: float32 [128, 128, 128], P('wide', 'narrow'), may hold values from -6 to 6
- phi_x: float32 [512, 128], replicated, may hold values from -0.5 to 0.5
- phi_y: float32 [512, 128], P('narrow'), may hold values from -0.5 to 0.5
- phi_z: float32 [128, 128], replicated, may hold values from -0.5 to 0.5
- log_trend: float32 [128, 512], P('wide', 'narrow'), may hold values from -0.3 to 3.3
Outputs:
- corrector: float32 [128, 512, 512], P('wide', 'narrow')
- residual: float32 [128, 512, 512], P('wide', 'narrow')
All inputs are finite; a program needn't handle non-finite values.
Results may differ from a plain program's by a relative error of at most 0.002.
Values sent between devices are 32-bit elements; how exact they have to be, the bound alone decides.
No kernel may reach another device: no remote copies, remote signals or barrier semaphores. Data moves between devices by JAX's collectives and lax.ppermute only.
A program may use at most 64 MiB of HBM per device.

v0:
```python
import jax
import jax.numpy as jnp
from jax import lax
from jax.sharding import PartitionSpec as P

ITERS = 4


def extended(cells, sides, width):
    for axis, dim in sides:
        count = lax.axis_size(axis)
        head = lax.slice_in_dim(cells, 0, width, axis=dim)
        tail = lax.slice_in_dim(cells, cells.shape[dim] - width, cells.shape[dim], axis=dim)
        cells = jnp.concatenate(
            [
                lax.ppermute(tail, axis, [(i, (i + 1) % count) for i in range(count)]),
                cells,
                lax.ppermute(head, axis, [((i + 1) % count, i) for i in range(count)]),
            ],
            axis=dim,
        )
    return cells


def harmonic(left, right):
    return 2.0 * left * right / (left + right)


def inner_sum(first, second):
    return lax.psum(jnp.sum(first * second), ("wide", "narrow"))


def local(coefficients, phi_x, phi_y, phi_z, log_trend):
    highest = lax.Precision.HIGHEST
    partial_x = jnp.einsum("kji,xi->kjx", coefficients, phi_x, precision=highest)
    partial_y = jnp.einsum(
        "kjx,yj->kyx",
        lax.all_gather(partial_x, "narrow", axis=1, tiled=True),
        phi_y,
        precision=highest,
    )
    widened = jnp.einsum(
        "zk,kyx->zyx",
        phi_z,
        lax.all_to_all(partial_y, "wide", split_axis=2, concat_axis=0, tiled=True),
        precision=highest,
    )
    log_field = lax.all_to_all(widened, "wide", split_axis=0, concat_axis=2, tiled=True)
    conductivity = jnp.exp(log_field + log_trend[:, :, None])
    padded = extended(conductivity, (("wide", 0), ("narrow", 1)), 1)
    center = padded[1:-1, 1:-1]
    face_z = harmonic(padded[:-1, 1:-1], padded[1:, 1:-1])
    face_y = harmonic(padded[1:-1, :-1], padded[1:-1, 1:])
    face_x = harmonic(center, jnp.roll(center, -1, 2))
    back_x = jnp.roll(face_x, 1, 2)
    diagonal = face_z[1:] + face_z[:-1] + face_y[:, 1:] + face_y[:, :-1] + face_x + back_x
    load = face_x - back_x
    corrector = jnp.zeros_like(load)
    residual = load
    scaled = residual / diagonal
    product_now = inner_sum(residual, scaled)
    direction = scaled
    for turn in range(ITERS):
        framed = extended(direction, (("wide", 0), ("narrow", 1)), 1)
        result = face_z[1:] * (direction - framed[2:, 1:-1]) + face_z[:-1] * (
            direction - framed[:-2, 1:-1]
        )
        result = (
            result
            + face_y[:, 1:] * (direction - framed[1:-1, 2:])
            + face_y[:, :-1] * (direction - framed[1:-1, :-2])
        )
        result = (
            result
            + face_x * (direction - jnp.roll(direction, -1, 2))
            + back_x * (direction - jnp.roll(direction, 1, 2))
        )
        alpha = product_now / lax.psum(jnp.sum(direction * result), ("wide", "narrow"))
        corrector = corrector + alpha * direction
        residual = residual - alpha * result
        scaled = residual / diagonal
        following = inner_sum(residual, scaled)
        direction = scaled + following / product_now * direction
        product_now = following
    return (corrector, residual)


def solution(mesh):
    placed = (P("wide", "narrow", None), P(), P("narrow", None), P(), P("wide", "narrow"))
    return jax.shard_map(
        local,
        mesh=mesh,
        in_specs=placed,
        out_specs=(P("wide", "narrow", None), P("wide", "narrow", None)),
        check_vma=False,
    )
```

profile of v0, /device:TPU:1, one launch (start us, length us, event | category | flops | bytes accessed | tf_op | source)
XLA Modules:
  0.0 981.0 jit_solution(17373108370793379451)
XLA Ops:
  2.7 19.8 %all_gather.3 = f32[2,128,512]{2,1,0:T(8,128)S(1)} all-gather(f32[2,16,512]{2,1,0:T(8,128)S(1)} %fusion.61), channel_id=1, replica_groups=mesh['wide'=64,'narrow'=8] {'narrow'}, dimensions={1}, use_global_device_ids=true | all-gather | bytes 589824 | tf_op jit(solution)/shard_map/all_gather | solution.py:38
  23.7 33.4 %all_to_all.36 = f32[64,1,1024]{2,1,0:T(1,128)S(1)} all-to-all(f32[64,1,1024]{2,1,0:T(1,128)S(1)} %reshape.8), channel_id=1, replica_groups=mesh['wide'=64,'narrow'=8] {'wide'}, dimensions={0} | all-to-all | bytes 524288 | tf_op jit(solution)/shard_map/all_to_all | solution.py:45
  61.2 24.6 %all_to_all.37 = f32[64,1,1024]{2,1,0:T(1,128)S(1)} all-to-all(f32[64,1,1024]{2,1,0:T(1,128)S(1)} %reshape.10), channel_id=1, replica_groups=mesh['wide'=64,'narrow'=8] {'wide'}, dimensions={0} | all-to-all | bytes 524288 | tf_op jit(solution)/shard_map/all_to_all | solution.py:48
  88.1 4.1 collective-permute-start
  92.1 4.6 collective-permute-start.1
  96.9 1.6 collective-permute-done
  98.5 1.5 collective-permute-done.1
  100.0 1.6 fusion.76
  101.7 1.6 copy.51
  103.7 5.0 collective-permute-start.3
  110.3 1.4 copy.52
  111.7 1.4 copy.54
  113.0 1.5 add_divide_fusion.1
  115.7 1.9 collective-permute-start.5
  117.6 7.4 collective-permute-start.4
  126.9 1.5 collective-permute-done.4
  129.1 1.7 fusion.75
  130.8 1.5 copy.55
  132.3 1.6 copy.57
  133.9 3.6 collective-permute-start.7
  137.5 3.4 collective-permute-done.6
  140.9 1.4 copy.56
  143.6 4.0 multiply_reduce_fusion.6
  147.6 105.3 %all-reduce = (f32[]{:T(128)}, f32[]{:T(128)}) all-reduce(f32[]{:T(128)} %get-tuple-element.9, f32[]{:T(128)} %get-tuple-element.8), channel_id=1, replica_groups=mesh['wide'=64,'narrow'=8] {'wide','narrow'}, use_global_device_ids=true, to_apply=%region_1.2 | all-reduce | flops 2 | bytes 16 | tf_op jit(solution)/shard_map/psum | solution.py:30
  254.2 2.9 multiply_reduce_fusion.5
  257.0 98.7 %psum.58 = f32[]{:T(128)} all-reduce(f32[]{:T(128)} %get-tuple-element.24), channel_id=1, replica_groups=mesh['wide'=64,'narrow'=8] {'wide','narrow'}, use_global_device_ids=true, to_apply=%region_5.6 | all-reduce | flops 1 | bytes 8 | tf_op jit(solution)/shard_map/psum | solution.py:30
  358.2 3.7 collective-permute-start.9
  361.9 4.9 collective-permute-start.8
  367.9 2.7 collective-permute-done.9
  372.3 1.7 fusion.74
  373.9 1.5 copy.59
  375.5 1.6 copy.61
  377.1 1.8 collective-permute-start.11
  378.9 3.3 collective-permute-done.10
  382.2 1.4 copy.60
  385.0 3.8 multiply_reduce_fusion.4
  388.8 105.1 %psum.59 = f32[]{:T(128)} all-reduce(f32[]{:T(128)} %get-tuple-element.22), channel_id=1, replica_groups=mesh['wide'=64,'narrow'=8] {'wide','narrow'}, use_global_device_ids=true, to_apply=%region_7.8 | all-reduce | flops 1 | bytes 8 | tf_op jit(solution)/shard_map/psum | solution.py:78
  495.2 2.9 multiply_reduce_fusion.3
  498.1 98.4 %psum.60 = f32[]{:T(128)} all-reduce(f32[]{:T(128)} %get-tuple-element.19), channel_id=1, replica_groups=mesh['wide'=64,'narrow'=8] {'wide','narrow'}, use_global_device_ids=true, to_apply=%region_9.10 | all-reduce | flops 1 | bytes 8 | tf_op jit(solution)/shard_map/psum | solution.py:30
  599.0 3.7 collective-permute-start.13
  602.7 4.9 collective-permute-start.12
  608.7 2.8 collective-permute-done.13
  613.1 1.7 fusion.73
  614.7 1.5 copy.63
  616.3 1.6 copy.65
  617.8 2.3 collective-permute-start.15
  620.1 3.4 collective-permute-done.14
  623.5 1.4 copy.64
  626.2 3.7 multiply_reduce_fusion.2
  629.9 104.6 %psum.61 = f32[]{:T(128)} all-reduce(f32[]{:T(128)} %get-tuple-element.17), channel_id=1, replica_groups=mesh['wide'=64,'narrow'=8] {'wide','narrow'}, use_global_device_ids=true, to_apply=%region_11.12 | all-reduce | flops 1 | bytes 8 | tf_op jit(solution)/shard_map/psum | solution.py:78
  735.9 3.0 multiply_reduce_fusion.1
  738.9 98.4 %psum.62 = f32[]{:T(128)} all-reduce(f32[]{:T(128)} %get-tuple-element.14), channel_id=1, replica_groups=mesh['wide'=64,'narrow'=8] {'wide','narrow'}, use_global_device_ids=true, to_apply=%region_13.14 | all-reduce | flops 1 | bytes 8 | tf_op jit(solution)/shard_map/psum | solution.py:30
  839.9 3.7 collective-permute-start.17
  843.6 5.1 collective-permute-start.16
  849.7 2.5 collective-permute-done.17
  853.9 1.7 fusion.72
  855.6 1.5 copy.67
  857.1 1.6 copy.69
  858.7 2.3 collective-permute-start.19
  861.7 2.6 collective-permute-done.18
  864.3 1.4 copy.68
  867.1 4.5 multiply_reduce_fusion
  871.5 104.6 %psum.63 = f32[]{:T(128)} all-reduce(f32[]{:T(128)} %get-tuple-element.12), channel_id=1, replica_groups=mesh['wide'=64,'narrow'=8] {'wide','narrow'}, use_global_device_ids=true, to_apply=%region_15.16 | all-reduce | flops 1 | bytes 8 | tf_op jit(solution)/shard_map/psum | solution.py:78
  977.5 1.7 multiply_subtract_fusion
  (91 shorter events, 34.7 us)
Async XLA Ops:
  0.6 1.0 copy-start
  2.7 19.8 %copy-start.11 = (f32[64,128]{1,0:T(8,128)S(1)}, f32[64,128]{1,0:T(8,128)}, u32[]{:S(2)}) copy-start(f32[64,128]{1,0:T(8,128)} %param.7) | copy-start | bytes 98308
  59.3 0.8 copy-start.10
  87.2 0.7 copy-start.12
  88.1 10.4 %collective-permute-start = (f32[1,64,512]{1,2,0:T(8,128)S(1)}, f32[1,64,512]{1,2,0:T(8,128)S(1)}, u32[]{:S(2)}, u32[]{:S(2)}) collective-permute-start(f32[1,64,512]{1,2,0:T(8,128)S(1)} %get-tuple-element.65), channel_id=1, source_target_pairs={{0,8},{8,16},{16,24},{24,32},{32,40},{40,48},{48,56},{56,64},{64,7... | collective-permute-start | bytes 393224 | tf_op jit(solution)/shard_map/ppermute | solution.py:16
  92.1 7.9 collective-permute-start.1
  101.7 1.6 copy-start.5
  103.7 8.0 collective-permute-start.3
  108.7 1.6 collective-permute-start.2
  115.6 138.5 %copy-start.3 = (f32[2,64,512]{1,2,0:T(8,128)}, f32[2,64,512]{1,2,0:T(8,128)S(1)}, u32[]{:S(2)}) copy-start(f32[2,64,512]{1,2,0:T(8,128)S(1)} %get-tuple-element.29) | copy-start | bytes 786436
  115.6 241.4 %copy-start.1 = (f32[2,64,512]{1,2,0:T(8,128)}, f32[2,64,512]{1,2,0:T(8,128)S(1)}, u32[]{:S(2)}) copy-start(f32[2,64,512]{1,2,0:T(8,128)S(1)} %get-tuple-element.28) | copy-start | bytes 786436
  115.7 11.2 %collective-permute-start.5 = (f32[1,64,512]{1,2,0:T(8,128)S(1)}, f32[1,64,512]{1,2,0:T(8,128)S(1)}, u32[]{:S(2)}, u32[]{:S(2)}) collective-permute-start(f32[1,64,512]{1,2,0:T(8,128)S(1)} %get-tuple-element.59), channel_id=1, source_target_pairs={{0,8},{8,16},{16,24},{24,32},{32,40},{40,48},{48,56},{56,64},{64,7... | collective-permute-start | bytes 393224 | tf_op jit(solution)/shard_map/ppermute | solution.py:16
  117.6 10.7 %collective-permute-start.4 = (f32[1,64,512]{1,2,0:T(8,128)S(1)}, f32[1,64,512]{1,2,0:T(8,128)S(1)}, u32[]{:S(2)}, u32[]{:S(2)}) collective-permute-start(f32[1,64,512]{1,2,0:T(8,128)S(1)} %get-tuple-element.60), channel_id=1, source_target_pairs={{8,0},{16,8},{24,16},{32,24},{40,32},{48,40},{56,48},{64,56},{72,6... | collective-permute-start | bytes 393224 | tf_op jit(solution)/shard_map/ppermute | solution.py:18
  128.3 0.7 copy-start.9
  133.9 8.4 collective-permute-start.7
  137.5 3.4 collective-permute-start.6
  358.2 12.4 %collective-permute-start.9 = (f32[1,64,512]{1,2,0:T(8,128)S(1)}, f32[1,64,512]{1,2,0:T(8,128)S(1)}, u32[]{:S(2)}, u32[]{:S(2)}) collective-permute-start(f32[1,64,512]{1,2,0:T(8,128)S(1)} %get-tuple-element.53), channel_id=1, source_target_pairs={{0,8},{8,16},{16,24},{24,32},{32,40},{40,48},{48,56},{56,64},{64,7... | collective-permute-start | bytes 393224 | tf_op jit(solution)/shard_map/ppermute | solution.py:16
  361.9 9.6 collective-permute-start.8
  371.5 0.7 copy-start.7
  377.1 6.6 collective-permute-start.11
  378.9 3.4 collective-permute-start.10
  385.0 110.2 %copy-start.4 = (f32[2,64,512]{1,2,0:T(8,128)S(1)}, f32[2,64,512]{1,2,0:T(8,128)}, u32[]{:S(2)}) copy-start(f32[2,64,512]{1,2,0:T(8,128)} %copy-done.3) | copy-start | bytes 786436
  599.0 12.4 %collective-permute-start.13 = (f32[1,64,512]{1,2,0:T(8,128)S(1)}, f32[1,64,512]{1,2,0:T(8,128)S(1)}, u32[]{:S(2)}, u32[]{:S(2)}) collective-permute-start(f32[1,64,512]{1,2,0:T(8,128)S(1)} %get-tuple-element.47), channel_id=1, source_target_pairs={{0,8},{8,16},{16,24},{24,32},{32,40},{40,48},{48,56},{56,64},{64,7... | collective-permute-start | bytes 393224 | tf_op jit(solution)/shard_map/ppermute | solution.py:16
  602.7 9.6 collective-permute-start.12
  612.3 0.7 copy-start.8
  617.8 7.0 collective-permute-start.15
  620.1 3.4 collective-permute-start.14
  839.8 13.3 %copy-start.2 = (f32[2,64,512]{1,2,0:T(8,128)}, f32[2,64,512]{1,2,0:T(8,128)S(1)}, u32[]{:S(2)}) copy-start(f32[2,64,512]{1,2,0:T(8,128)S(1)} %multiply_add_fusion.1) | copy-start | bytes 786436
  839.9 12.4 %collective-permute-start.17 = (f32[1,64,512]{1,2,0:T(8,128)S(1)}, f32[1,64,512]{1,2,0:T(8,128)S(1)}, u32[]{:S(2)}, u32[]{:S(2)}) collective-permute-start(f32[1,64,512]{1,2,0:T(8,128)S(1)} %get-tuple-element.41), channel_id=1, source_target_pairs={{0,8},{8,16},{16,24},{24,32},{32,40},{40,48},{48,56},{56,64},{64,7... | collective-permute-start | bytes 393224 | tf_op jit(solution)/shard_map/ppermute | solution.py:16
  843.6 9.6 collective-permute-start.16
  853.1 0.7 copy-start.6
  858.7 7.0 collective-permute-start.19
  860.9 3.4 collective-permute-start.18
where the time goes:
time: 983 us; the launch traced here: 981 us
  blocking collectives  793 us (81%)
  starting transfers between devices  59.8 us (6%)
  local copies, waits for them, and re-layouts  51 us (5%)
  other arithmetic  35.6 us (4%)
  waiting for transfers between devices  29.3 us (3%)
  between operations  10.5 us (1%)
    psum x4, blocking collectives, inner_sum(): return lax.psum(jnp.sum(first * second), ('wide', 'narrow'))  401 us
    psum x3, blocking collectives, local(): lax.psum(jnp.sum(direction * result), ('wide', 'narrow'))  314 us
    all_to_all x1, blocking collectives, local(): lax.all_to_all(partial_y, 'wide', split_axis=2, concat_axis=0, tiled=True)  33.4 us
    ppermute x10, starting transfers between devices, extended(): lax.ppermute(head, axis, [((i + 1) % count, i) for i in range(count)])  32 us
    ppermute x10, starting transfers between devices, extended(): lax.ppermute(tail, axis, [(i, (i + 1) % count) for i in range(count)])  27.7 us
    all_to_all x1, blocking collectives, local(): lax.all_to_all(widened, 'wide', split_axis=0, concat_axis=2, tiled=True)  24.6 us
    all_gather x1, blocking collectives, local(): lax.all_gather(partial_x, 'narrow', axis=1, tiled=True)  19.8 us
  transfers between devices with their start and end apart: 20, of which 15 were waited for; matrix products, arithmetic and copies ran while one was open for 1% of the time, Pallas kernels for 0%

commit v1 on v0

v1 whole, which is shorter than its diff:
```python
import functools

import jax
import jax.numpy as jnp
from jax import lax
from jax.experimental import pallas as pl
from jax.experimental.pallas import tpu as pltpu
from jax.sharding import Mesh
from jax.sharding import PartitionSpec as P

ITERS = 4
DEPTH = ITERS + 1
PLANES = 2 + 2 * DEPTH
ROWS = 80
NX = 512
PARCEL = 56
GRAM = [(i, j) for i in range(ITERS + 1) for j in range(i, ITERS + 1) if i < ITERS]
BF16 = jnp.bfloat16
F32 = jnp.float32
VMEM_LIMIT = 56 * 1024 * 1024


def iota(shape, dim):
    return lax.broadcasted_iota(jnp.int32, shape, dim)


def split2(a):
    high = a.astype(BF16)
    return high, (a - high.astype(F32)).astype(BF16)


def split3(a):
    high = a.astype(BF16)
    rest = a - high.astype(F32)
    middle = rest.astype(BF16)
    return high, middle, (rest - middle.astype(F32)).astype(BF16)


def mm(a, b):
    return jnp.dot(a, b, preferred_element_type=F32)


def pick_left(chosen, a):
    return sum(mm(chosen, part) for part in split3(a))


def pick_right(a, chosen):
    return sum(mm(part, chosen) for part in split3(a))


def dot3(a, b):
    (ah, al), (bh, bl) = a, b
    return mm(ah, bh) + (mm(al, bh) + mm(ah, bl))


def one_hot(condition):
    return jnp.where(condition, 1.0, 0.0).astype(BF16)


def pack_kernel(coef_ref, trend_ref, out_ref):
    trend = jnp.concatenate([trend_ref[0:1, :], trend_ref[1:2, :]], axis=1)
    for quarter in range(4):
        rows = []
        for r in range(2):
            for jj in range(4):
                at = 4 * quarter + jj
                rows.append(coef_ref[r, at : at + 1, :])
        rows.append(trend)
        for z in range(16):
            for s, row in enumerate(rows):
                out_ref[(quarter * 16 + z) * 9 + s] = row


def planes_kernel(got_ref, phi_z_ref, phi_y_ref, out_ref):
    y, z = lax.axis_index("y"), lax.axis_index("z")
    modes = []
    rest = []
    edges = []
    s1 = iota((PARCEL, 128), 0)
    k1 = iota((PARCEL, 128), 1)
    s9 = iota((PARCEL, 576), 0)
    row = iota((PARCEL, 576), 1)
    source = (row * 7282) >> 16
    part = row - 9 * source
    s6 = iota((PARCEL, 64), 0)
    e6 = iota((PARCEL, 64), 1)
    edge = 4 * y + s6 - 50
    edge = jnp.where(edge < 8, edge, edge + 48)
    edge_pick = one_hot((s6 >= 50) & (s6 < 54) & (e6 == edge))
    same_mode = (part < 8) & ((part & 3) == (s9 & 3)) & (s9 < 48)
    for to in range(4):
        plane = (2 * (16 * to + z) - DEPTH + (s1 >> 2)) & 127
        modes.append(one_hot((plane == k1) & (s1 < 48)))
        wide = (16 * to + z - 3 + 2 * y + s9 - 48) & 63
        rest.append(one_hot((part == 8) & (source == wide) & (s9 >= 48) & (s9 < 50)))
        edges.append(edge_pick)
    modes = jnp.concatenate(modes, axis=0)
    phi = split2(pick_left(modes, phi_z_ref[...]))
    k2 = iota((128, 576), 0)
    r2 = iota((128, 576), 1)
    src2 = (r2 * 7282) >> 16
    part2 = r2 - 9 * src2
    spread = one_hot((k2 == 2 * src2 + (part2 >> 2)) & (part2 < 8))
    keep = jnp.concatenate([same_mode] * 4, axis=0)
    high = jnp.where(keep, mm(phi[0], spread), 0.0).astype(BF16)
    low = jnp.where(keep, mm(phi[1], spread), 0.0).astype(BF16)
    high = high + jnp.concatenate(rest, axis=0)
    got = split2(got_ref[...])
    result = dot3((high, low), got)
    edge_rows = pick_left(edge_pick, phi_y_ref[...])
    for to in range(4):
        block = result[to * PARCEL : (to + 1) * PARCEL] + edge_rows
        for x in range(4):
            out_ref[to * 4 + x] = block


def roll_x(a, shift):
    return pltpu.roll(a, shift % NX, 1)


def solve_kernel(
    all_ref, phi_y_ref, phi_x_ref,
    t0_out, t1_out, t2_out, t3_out, t4_out, diag_out, gram_out,
    rec, fx, fy, fz, dinv, t0, t1, t2, t3, phi_xt,
):
    x, c = lax.axis_index("x"), lax.axis_index("c")
    n = 2 * x + c

    tail = all_ref[:, 48:56, :].reshape(256, 128)
    h = iota((16, 256), 0)
    col = iota((16, 256), 1)
    edge = jnp.where(h < 8, h + 8, h - 8)
    other = jnp.where(h < 8, n + 7, n + 1) & 7
    want = (((other & 1) * 16 + (edge >> 2) * 4 + (other >> 1)) * 8) + 2 + (edge & 3)
    halo = pick_left(one_hot(col == want), tail)
    phi_ext = jnp.concatenate([halo[0:8], phi_y_ref[...], halo[8:16]], axis=0)

    tail_t = tail.T
    a = iota((256, 48), 0)
    b = iota((256, 48), 1)
    src, s = a >> 3, a & 7
    a_n = 2 * (src & 3) + (src >> 4)
    q = 2 * ((src >> 2) & 3) + s
    p = b & 15
    group = b >> 4
    from_n = jnp.where(group == 0, n, jnp.where(group == 1, n + 7, n + 1)) & 7
    right = (s < 2) & (a_n == from_n)
    trend = pick_right(tail_t[0:64], one_hot(right & (2 * q == p + 1))) + pick_right(
        tail_t[64:128], one_hot(right & (2 * q + 1 == p + 1))
    )
    trend = jnp.concatenate([trend[56:64, 16:32], trend[:, 0:16], trend[0:8, 32:48]], axis=0)

    j = iota((128, 256), 0)
    col = iota((128, 256), 1)
    src = col >> 3
    col_j = 16 * (2 * (src & 3) + (src >> 4)) + 4 * ((src >> 2) & 3) + (col & 3)
    order = one_hot(j == col_j)
    second = (iota((ROWS, 256), 1) >> 2) & 1
    lift = []
    for half in split2(phi_ext):
        spread = mm(half, order)
        lift.append(
            jnp.concatenate(
                [jnp.where(second == 0, spread, 0.0), jnp.where(second == 1, spread, 0.0)], axis=0
            ).astype(BF16)
        )
    for part in range(2):
        phi_xt[part] = split2(phi_x_ref[...].T)[part]
    for pair in range(PLANES // 2):
        block = all_ref[:, 8 * pair : 8 * pair + 8, :].reshape(256, 128)
        rows = dot3(tuple(lift), split2(block))
        for half in range(2):
            log_field = dot3(split2(rows[half * ROWS : (half + 1) * ROWS]), (phi_xt[0], phi_xt[1]))
            plane = 2 * pair + half
            rec[plane] = jnp.exp(-(log_field + trend[:, plane : plane + 1]))

    blocks = ROWS // 8
    sub = iota((8, NX), 0)

    def rows_of(ref, plane, block):
        return ref[plane, 8 * block : 8 * block + 8, :]

    def ahead(now, following):
        return jnp.where(sub == 7, pltpu.roll(following, 7, 0), pltpu.roll(now, 7, 0))

    def behind(now, previous):
        return jnp.where(sub == 0, pltpu.roll(previous, 1, 0), pltpu.roll(now, 1, 0))

    def inverse(a):
        return pl.reciprocal(a, approx=False)

    for block in range(blocks):
        fz[0, 8 * block : 8 * block + 8, :] = 2.0 * inverse(rows_of(rec, 0, block) + rows_of(rec, 1, block))

    def faces(plane, carry):
        last_y = None
        now = rows_of(rec, plane, 0)
        for block in range(blocks):
            at = slice(8 * block, 8 * block + 8)
            following = rows_of(rec, plane, min(block + 1, blocks - 1))
            face_x = 2.0 * inverse(now + roll_x(now, -1))
            face_y = 2.0 * inverse(now + ahead(now, following))
            face_z = 2.0 * inverse(now + rec[plane + 1, at, :])
            fx[plane, at, :] = face_x
            fy[plane, at, :] = face_y
            fz[plane, at, :] = face_z
            back_x = roll_x(face_x, 1)
            back_y = behind(face_y, face_y if last_y is None else last_y)
            diagonal = face_z + fz[plane - 1, at, :] + face_y + back_y + face_x + back_x
            inv = inverse(diagonal)
            dinv[plane, at, :] = inv
            t0[plane, at, :] = (face_x - back_x) * inv
            last_y = face_y
            now = following
        return carry

    lax.fori_loop(1, PLANES - 1, faces, 0)

    def neighbours(field, plane, block, now, previous, following, last_flux):
        at = slice(8 * block, 8 * block + 8)
        face_x = fx[plane, at, :]
        face_y = fy[plane, at, :]
        flux_y = face_y * now
        total = face_x * roll_x(now, -1) + roll_x(face_x * now, 1)
        total = total + face_y * ahead(now, following)
        total = total + behind(flux_y, flux_y if last_flux is None else last_flux)
        total = total + fz[plane, at, :] * field[plane + 1, at, :]
        total = total + fz[plane - 1, at, :] * field[plane - 1, at, :]
        return total * dinv[plane, at, :], flux_y

    def sweep(field, older, target, first, last):
        def one(plane, carry):
            flux = None
            now = rows_of(field, plane, 0)
            for block in range(blocks):
                at = slice(8 * block, 8 * block + 8)
                following = rows_of(field, plane, min(block + 1, blocks - 1))
                value, flux = neighbours(field, plane, block, now, None, following, flux)
                if older is not None:
                    value = 2.0 * value - older[plane, at, :]
                target[plane, at, :] = value
                now = following
            return carry

        lax.fori_loop(first, last, one, 0)

    sweep(t0, None, t1, 2, PLANES - 2)
    sweep(t1, t0, t2, 3, PLANES - 3)
    sweep(t2, t1, t3, 4, PLANES - 4)

    def own(index, sums):
        plane = DEPTH + index
        sums = list(sums)
        before = rows_of(t3, plane, 0)
        flux = rows_of(fy, plane, 0) * before
        now = rows_of(t3, plane, 1)
        for block in range(1, blocks - 1):
            at = slice(8 * block, 8 * block + 8)
            to = slice(8 * block - 8, 8 * block)
            following = rows_of(t3, plane, block + 1)
            value, flux = neighbours(t3, plane, block, now, None, following, flux)
            basis = [t0[plane, at, :], t1[plane, at, :], t2[plane, at, :], now]
            basis.append(2.0 * value - basis[2])
            diagonal = inverse(dinv[plane, at, :])
            for ref, field in zip((t0_out, t1_out, t2_out, t3_out, t4_out), basis):
                ref[index, to, :] = field
            diag_out[index, to, :] = diagonal
            weighted = [diagonal * field for field in basis[:ITERS]]
            for at_sum, (i, k) in enumerate(GRAM):
                product = weighted[i] * basis[k]
                product = (product[:, 0:128] + product[:, 128:256]) + (product[:, 256:384] + product[:, 384:512])
                sums[at_sum] = sums[at_sum] + product
            now = following
        return tuple(sums)

    sums = lax.fori_loop(0, 2, own, tuple(jnp.zeros((8, 128), F32) for _ in GRAM))
    lane = iota((1, 128), 1)
    gram = jnp.zeros((1, 128), F32)
    for at_sum, value in enumerate(sums):
        value = jnp.sum(jnp.sum(value, axis=0, keepdims=True), axis=1, keepdims=True)
        gram = gram + jnp.where(lane == at_sum, value, 0.0)
    for to in range(32):
        gram_out[to] = gram


def relay_kernel(got_ref, out_ref):
    total = jnp.zeros((1, 128), F32)
    for source in range(32):
        total = total + got_ref[source]
    for to in range(16):
        out_ref[to] = total


def combine_kernel(got_ref, t0, t1, t2, t3, t4, diag, corrector, residual):
    total = jnp.zeros((1, 128), F32)
    for source in range(16):
        total = total + got_ref[source]
    lane = iota((1, 128), 1)
    gram = {}
    for at_sum, (i, k) in enumerate(GRAM):
        value = jnp.sum(jnp.where(lane == at_sum, total, 0.0), axis=1, keepdims=True)
        gram[i, k] = gram[k, i] = jnp.broadcast_to(value, (8, 128))
    zero = jnp.zeros((8, 128), F32)

    def shifted(a):
        return [
            0.5 * a[1],
            a[0] + 0.5 * a[2],
            0.5 * (a[1] + a[3]),
            0.5 * (a[2] + a[4]),
            0.5 * a[3],
        ]

    def paired(a, b):
        result = zero
        for i in range(ITERS + 1):
            for k in range(ITERS + 1):
                if (i, k) in gram and a[i] is not zero and b[k] is not zero:
                    result = result + a[i] * gram[i, k] * b[k]
        return result

    scaled = [jnp.ones((8, 128), F32)] + [zero] * ITERS
    direction = list(scaled)
    answer = [zero] * (ITERS + 1)
    product = gram[0, 0]
    for turn in range(ITERS):
        moved = shifted(direction)
        image = [
            zero if k > turn + 1 else direction[k] - moved[k] for k in range(ITERS + 1)
        ]
        alpha = product / paired(direction, image)
        answer = [
            zero if k > turn else answer[k] + alpha * direction[k] for k in range(ITERS + 1)
        ]
        scaled = [
            zero if k > turn + 1 else scaled[k] - alpha * image[k] for k in range(ITERS + 1)
        ]
        if turn < ITERS - 1:
            following = paired(scaled, scaled)
            beta = following / product
            direction = [
                zero if k > turn + 1 else scaled[k] + beta * direction[k] for k in range(ITERS + 1)
            ]
            product = following
    for plane in range(2):
        for block in range(8):
            for group in range(4):
                at = (plane, slice(8 * block, 8 * block + 8), slice(128 * group, 128 * group + 128))
                basis = [t0[at], t1[at], t2[at], t3[at], t4[at]]
                first = answer[0] * basis[0]
                second = scaled[0] * basis[0]
                for k in range(1, ITERS + 1):
                    if k < ITERS:
                        first = first + answer[k] * basis[k]
                    second = second + scaled[k] * basis[k]
                corrector[at] = first
                residual[at] = diag[at] * second


def call(kernel, out_shapes, scratch=()):
    return pl.pallas_call(
        kernel,
        out_shape=out_shapes,
        scratch_shapes=scratch,
        compiler_params=pltpu.CompilerParams(vmem_limit_bytes=VMEM_LIMIT),
    )


def array(*shape):
    return jax.ShapeDtypeStruct(shape, F32)


def local(coefficients, phi_x, phi_y, phi_z, log_trend):
    packed = call(pack_kernel, array(576, 1, 128))(coefficients, log_trend)
    got = lax.all_to_all(packed, ("y", "z"), 0, 0, tiled=True).reshape(576, 128)
    parcels = call(planes_kernel, array(16, PARCEL, 128))(got, phi_z, phi_y)
    parcels = lax.all_to_all(parcels, ("y", "x"), 0, 0, tiled=True)
    parcels = lax.all_gather(parcels, "c", tiled=True)
    own = array(2, 64, NX)
    field = pltpu.VMEM((PLANES, ROWS, NX), F32)
    *basis, diagonal, gram = call(
        solve_kernel,
        [own] * 6 + [array(32, 1, 128)],
        [field] * 9 + [pltpu.VMEM((2, 128, NX), BF16)],
    )(parcels, phi_y, phi_x)
    gram = lax.all_to_all(gram, ("y", "x", "c"), 0, 0, tiled=True)
    gram = call(relay_kernel, array(16, 1, 128))(gram)
    gram = lax.all_to_all(gram, "z", 0, 0, tiled=True)
    return tuple(call(combine_kernel, [own, own])(gram, *basis, diagonal))


def solution(mesh):
    chips = Mesh(mesh.devices.reshape(4, 16, 4, 2), ("y", "z", "x", "c"))
    wide, narrow = ("y", "z"), ("x", "c")
    return jax.shard_map(
        local,
        mesh=chips,
        in_specs=(P(wide, narrow, None), P(), P(narrow, None), P(), P(wide, narrow)),
        out_specs=(P(wide, narrow, None), P(wide, narrow, None)),
        check_vma=False,
    )
```

time: 983 us -> 108 us (0.11)
  blocking collectives: 793 us -> 88.1 us
  starting transfers between devices: 59.8 us -> 0 us
  local copies, waits for them, and re-layouts: 51 us -> 0 us
  other arithmetic: 35.6 us -> 0 us
  waiting for transfers between devices: 29.3 us -> 0 us
  Pallas kernels: 0 us -> 18.3 us
  between operations: 10.5 us -> 0.63 us
    psum x7 -> x0, blocking collectives: 715 us -> none  [the longest x4 401 us: inner_sum(): return lax.psum(jnp.sum(first * second), ('wide', 'narrow'))]
    ppermute x20 -> x0, starting transfers between devices: 59.8 us -> none  [the longest x10 32 us: extended(): lax.ppermute(head, axis, [((i + 1) % count, i) for i in range(count)])]
    ppermute x20 -> x0, waiting for transfers between devices: 29.3 us -> none  [the longest x10 18.2 us: extended(): lax.ppermute(head, axis, [((i + 1) % count, i) for i in range(count)])]
    slice x31 -> x0, local copies, waits for them, and re-layouts: 27.8 us -> none  [the longest x9 13.2 us: extended(): head = lax.slice_in_dim(cells, 0, width, axis=dim)]
    reduce_sum x7 -> x0, other arithmetic: 24.7 us -> none  [the longest x4 15.9 us: local(): jnp.sum(direction * result)]
    all_to_all x2 -> x4, blocking collectives: 58 us -> 81.2 us  [the longest x1 39.4 us: local(): got = lax.all_to_all(packed, ('y', 'z'), 0, 0, tiled=True).reshape(576, 128)]
    pallas_call x0 -> x5, Pallas kernels: none -> 18.3 us  [the longest x1 10.3 us: local(): call(solve_kernel, [own] * 6 + [array(32, 1, 128)], [field] * 9 + [pltpu....]
    ppermute x10 -> x0, local copies, waits for them, and re-layouts: 13.7 us -> none  [the longest x5 6.93 us: extended(): lax.ppermute(head, axis, [((i + 1) % count, i) for i in range(count)])]
  transfers between devices with their start and end apart: 20 -> 0, of which waited for: 15 -> 0; matrix products, arithmetic and copies ran while one was open for 1% -> 0% of each run, Pallas kernels for 0% -> 0%
where the time goes in v1:
time: 108 us; the launch traced here: 107 us
  blocking collectives  88.1 us (82%)
  Pallas kernels  18.3 us (17%)
    all_to_all x1, blocking collectives, local(): got = lax.all_to_all(packed, ('y', 'z'), 0, 0, tiled=True).reshape(576, 128)  39.4 us
    all_to_all x1, blocking collectives, local(): parcels = lax.all_to_all(parcels, ('y', 'x'), 0, 0, tiled=True)  15.3 us
    all_to_all x1, blocking collectives, local(): gram = lax.all_to_all(gram, 'z', 0, 0, tiled=True)  15.2 us
    all_to_all x1, blocking collectives, local(): gram = lax.all_to_all(gram, ('y', 'x', 'c'), 0, 0, tiled=True)  11.3 us
    pallas_call x1, Pallas kernels, local(): call(solve_kernel, [own] * 6 + [array(32, 1, 128)], [field] * 9 + [pltpu....  10.3 us
    all_gather x1, blocking collectives, local(): parcels = lax.all_gather(parcels, 'c', tiled=True)  6.88 us
    pallas_call x1, Pallas kernels, local(): parcels = call(planes_kernel, array(16, PARCEL, 128))(got, phi_z, phi_y)  2.56 us
    pallas_call x1, Pallas kernels, local(): return tuple(call(combine_kernel, [own, own])(gram, *basis, diagonal))  2.52 us

profile of v1, /device:TPU:1, one launch (start us, length us, event | category | flops | bytes accessed | tf_op | source)
XLA Modules:
  0.0 107.0 jit_solution(15055183678232338278)
XLA Ops:
  0.6 1.6 %shard_map.68 = f32[576,1,128]{2,1,0:T(1,128)} custom-call(f32[2,16,128]{2,1,0:T(8,128)} %coef_ref.1, f32[2,64]{1,0:T(2,128)} %trend_ref.1), custom_call_target="tpu_custom_call" | custom-call | tf_op jit(solution)/shard_map/pallas_call | solution.py:374
  2.2 39.4 %all_to_all.20 = f32[576,1,128]{2,1,0:T(1,128)} all-to-all(f32[576,1,128]{2,1,0:T(1,128)} %shard_map.68), channel_id=1, replica_groups=mesh['y'=4,'z'=16,'x'=4,'c'=2] {'y','z'}, dimensions={0} | all-to-all | bytes 589824 | tf_op jit(solution)/shard_map/all_to_all | solution.py:375
  41.6 2.6 %shard_map.69 = f32[16,56,128]{2,1,0:T(8,128)} custom-call(f32[576,128]{1,0:T(8,128)} %bitcast.1, f32[128,128]{1,0:T(8,128)} %phi_z_ref.1, f32[64,128]{1,0:T(8,128)} %phi_y_ref.3), custom_call_target="tpu_custom_call" | custom-call | tf_op jit(solution)/shard_map/pallas_call | solution.py:376
  44.2 15.3 %all_to_all.21 = f32[16,56,128]{2,1,0:T(8,128)S(1)} all-to-all(f32[16,56,128]{2,1,0:T(8,128)} %shard_map.69), channel_id=1, replica_groups=mesh['y'=4,'z'=16,'x'=4,'c'=2] {'y','x'}, dimensions={0} | all-to-all | bytes 917504 | tf_op jit(solution)/shard_map/all_to_all | solution.py:377
  59.5 6.9 %all_gather.3.all_ref = f32[32,56,128]{2,1,0:T(8,128)} all-gather(f32[16,56,128]{2,1,0:T(8,128)S(1)} %all_to_all.21), channel_id=1, replica_groups=mesh['y'=4,'z'=16,'x'=4,'c'=2] {'c'}, dimensions={0}, use_global_device_ids=true | all-gather | bytes 1376256 | tf_op jit(solution)/shard_map/all_gather | solution.py:378
  66.3 10.3 %shard_map.70 = (f32[2,64,512]{2,1,0:T(8,128)}, f32[2,64,512]{2,1,0:T(8,128)}, f32[2,64,512]{2,1,0:T(8,128)}, f32[2,64,512]{2,1,0:T(8,128)}, f32[2,64,512]{2,1,0...) custom-call(f32[32,56,128]{2,1,0:T(8,128)} %all_gather.3.all_ref, f32[64,128]{1,0:T(8,128)} %phi_y_ref.3, ...), custom_call_target="tpu_custom_call" | custom-call | tf_op jit(solution)/shard_map/pallas_call | solution.py:381
  76.6 11.3 %all_to_all.22.got_ref = f32[32,1,128]{2,1,0:T(1,128)} all-to-all(f32[32,1,128]{2,1,0:T(1,128)} %get-tuple-element.9), channel_id=1, replica_groups=mesh['y'=4,'z'=16,'x'=4,'c'=2] {'y','x','c'}, dimensions={0} | all-to-all | bytes 32768 | tf_op jit(solution)/shard_map/all_to_all | solution.py:386
  87.9 1.4 %shard_map.71 = f32[16,1,128]{2,1,0:T(1,128)} custom-call(f32[32,1,128]{2,1,0:T(1,128)} %all_to_all.22.got_ref), custom_call_target="tpu_custom_call" | custom-call | tf_op jit(solution)/shard_map/pallas_call | solution.py:387
  89.3 15.2 %all_to_all.23.got_ref = f32[16,1,128]{2,1,0:T(1,128)} all-to-all(f32[16,1,128]{2,1,0:T(1,128)} %shard_map.71), channel_id=1, replica_groups=mesh['y'=4,'z'=16,'x'=4,'c'=2] {'z'}, dimensions={0} | all-to-all | bytes 16384 | tf_op jit(solution)/shard_map/all_to_all | solution.py:388
  104.5 2.5 %shard_map.72 = (f32[2,64,512]{2,1,0:T(8,128)}, f32[2,64,512]{2,1,0:T(8,128)}) custom-call(f32[16,1,128]{2,1,0:T(1,128)} %all_to_all.23.got_ref, f32[2,64,512]{2,1,0:T(8,128)} %get-tuple-element.10.t0, f32[2,64,512]{2,1,0:T(8,128)} %get-tuple-element.11.t1, f32[2,64,512]{2,1,0:T(8,128)} %get-tuple-element.12.t2, f32[2,64,512]{2,1,0:T(8,128)} %get-tuple-element.13.t3, ...), custom_call_target="tpu_custom_call" | custom-call | tf_op jit(solution)/shard_map/pallas_call | solution.py:389

commit v2 on v1

--- a/solution.py
+++ b/solution.py
@@ -17,7 +17,6 @@
 GRAM = [(i, j) for i in range(ITERS + 1) for j in range(i, ITERS + 1) if i < ITERS]
 BF16 = jnp.bfloat16
 F32 = jnp.float32
-VMEM_LIMIT = 56 * 1024 * 1024
 
 
 def iota(shape, dim):
@@ -357,12 +356,15 @@
                 residual[at] = diag[at] * second
 
 
-def call(kernel, out_shapes, scratch=()):
+def call(kernel, n_in, out_shapes, scratch=(), mebibytes=8):
+    near = pl.BlockSpec(memory_space=pltpu.VMEM)
     return pl.pallas_call(
         kernel,
+        in_specs=[near] * n_in,
+        out_specs=[near] * len(out_shapes) if isinstance(out_shapes, list) else near,
         out_shape=out_shapes,
         scratch_shapes=scratch,
-        compiler_params=pltpu.CompilerParams(vmem_limit_bytes=VMEM_LIMIT),
+        compiler_params=pltpu.CompilerParams(vmem_limit_bytes=mebibytes * 1024 * 1024),
     )
 
 
@@ -371,22 +373,24 @@
 
 
 def local(coefficients, phi_x, phi_y, phi_z, log_trend):
-    packed = call(pack_kernel, array(576, 1, 128))(coefficients, log_trend)
+    packed = call(pack_kernel, 2, array(576, 1, 128))(coefficients, log_trend)
     got = lax.all_to_all(packed, ("y", "z"), 0, 0, tiled=True).reshape(576, 128)
-    parcels = call(planes_kernel, array(16, PARCEL, 128))(got, phi_z, phi_y)
+    parcels = call(planes_kernel, 3, array(16, PARCEL, 128))(got, phi_z, phi_y)
     parcels = lax.all_to_all(parcels, ("y", "x"), 0, 0, tiled=True)
     parcels = lax.all_gather(parcels, "c", tiled=True)
     own = array(2, 64, NX)
     field = pltpu.VMEM((PLANES, ROWS, NX), F32)
     *basis, diagonal, gram = call(
         solve_kernel,
+        3,
         [own] * 6 + [array(32, 1, 128)],
         [field] * 9 + [pltpu.VMEM((2, 128, NX), BF16)],
+        32,
     )(parcels, phi_y, phi_x)
     gram = lax.all_to_all(gram, ("y", "x", "c"), 0, 0, tiled=True)
-    gram = call(relay_kernel, array(16, 1, 128))(gram)
+    gram = call(relay_kernel, 1, array(16, 1, 128))(gram)
     gram = lax.all_to_all(gram, "z", 0, 0, tiled=True)
-    return tuple(call(combine_kernel, [own, own])(gram, *basis, diagonal))
+    return tuple(call(combine_kernel, 7, [own, own])(gram, *basis, diagonal))
 
 
 def solution(mesh):

time: 108 us -> 98.4 us (0.911)
  Pallas kernels: 18.3 us -> 10.3 us
  blocking collectives: 88.1 us -> 85.7 us
  local copies, waits for them, and re-layouts: 0 us -> 1.41 us
    pallas_call x5, Pallas kernels: 18.3 us -> 10.3 us  [the longest x1 8.12 us: local(): call(solve_kernel, 3, [own] * 6 + [array(32, 1, 128)], [field] * 9 + [plt...]
    unnamed x0 -> x10, local copies, waits for them, and re-layouts: none -> 1.41 us
where the time goes in v2:
time: 98.4 us; the launch traced here: 98 us
  blocking collectives  85.7 us (87%)
  Pallas kernels  10.3 us (10%)
  local copies, waits for them, and re-layouts  1.41 us (1%)
    all_to_all x1, blocking collectives, local(): got = lax.all_to_all(packed, ('y', 'z'), 0, 0, tiled=True).reshape(576, 128)  39.2 us
    all_to_all x1, blocking collectives, local(): parcels = lax.all_to_all(parcels, ('y', 'x'), 0, 0, tiled=True)  15.1 us
    all_to_all x1, blocking collectives, local(): gram = lax.all_to_all(gram, 'z', 0, 0, tiled=True)  14.2 us
    all_to_all x1, blocking collectives, local(): gram = lax.all_to_all(gram, ('y', 'x', 'c'), 0, 0, tiled=True)  10.3 us
    pallas_call x1, Pallas kernels, local(): call(solve_kernel, 3, [own] * 6 + [array(32, 1, 128)], [field] * 9 + [plt...  8.12 us
    all_gather x1, blocking collectives, local(): parcels = lax.all_gather(parcels, 'c', tiled=True)  6.83 us

profile of v2, /device:TPU:1, one launch (start us, length us, event | category | flops | bytes accessed | tf_op | source)
XLA Modules:
  0.0 98.0 jit_solution(13449682676631660228)
XLA Ops:
  0.6 0.0 copy-start.3
  0.6 0.7 copy-done.3
  1.3 0.0 copy-start.4
  1.4 0.7 copy-done.4
  2.0 0.2 shard_map.68
  2.2 0.0 copy-start.1
  2.2 0.0 copy-start.2
  2.2 39.2 %all_to_all.20 = f32[576,1,128]{2,1,0:T(1,128)S(1)} all-to-all(f32[576,1,128]{2,1,0:T(1,128)S(1)} %shard_map.68), channel_id=1, replica_groups=mesh['y'=4,'z'=16,'x'=4,'c'=2] {'y','z'}, dimensions={0} | all-to-all | bytes 589824 | tf_op jit(solution)/shard_map/all_to_all | solution.py:377
  41.4 0.0 copy-done.1
  41.5 0.0 copy-done.2
  41.5 0.8 shard_map.69
  42.3 15.1 %all_to_all.21 = f32[16,56,128]{2,1,0:T(8,128)S(1)} all-to-all(f32[16,56,128]{2,1,0:T(8,128)S(1)} %shard_map.69), channel_id=1, replica_groups=mesh['y'=4,'z'=16,'x'=4,'c'=2] {'y','x'}, dimensions={0} | all-to-all | bytes 917504 | tf_op jit(solution)/shard_map/all_to_all | solution.py:379
  57.4 0.0 copy-start
  57.4 6.8 %all_gather.3.all_ref = f32[32,56,128]{2,1,0:T(8,128)S(1)} all-gather(f32[16,56,128]{2,1,0:T(8,128)S(1)} %all_to_all.21), channel_id=1, replica_groups=mesh['y'=4,'z'=16,'x'=4,'c'=2] {'c'}, dimensions={0}, use_global_device_ids=true | all-gather | bytes 1376256 | tf_op jit(solution)/shard_map/all_gather | solution.py:380
  64.2 0.0 copy-done
  64.2 8.1 %shard_map.70 = (f32[2,64,512]{2,1,0:T(8,128)S(1)}, f32[2,64,512]{2,1,0:T(8,128)S(1)}, f32[2,64,512]{2,1,0:T(8,128)S(1)}, f32[2,64,512]{2,1,0:T(8,128)S(1)}, f32...) custom-call(f32[32,56,128]{2,1,0:T(8,128)S(1)} %all_gather.3.all_ref, ...), custom_call_target="tpu_custom_call" | custom-call | tf_op jit(solution)/shard_map/pallas_call | solution.py:383
  72.3 10.3 %all_to_all.22.got_ref = f32[32,1,128]{2,1,0:T(1,128)S(1)} all-to-all(f32[32,1,128]{2,1,0:T(1,128)S(1)} %get-tuple-element.9), channel_id=1, replica_groups=mesh['y'=4,'z'=16,'x'=4,'c'=2] {'y','x','c'}, dimensions={0} | all-to-all | bytes 32768 | tf_op jit(solution)/shard_map/all_to_all | solution.py:390
  82.7 14.2 %all_to_all.23.got_ref = f32[16,1,128]{2,1,0:T(1,128)S(1)} all-to-all(f32[16,1,128]{2,1,0:T(1,128)S(1)} %shard_map.71), channel_id=1, replica_groups=mesh['y'=4,'z'=16,'x'=4,'c'=2] {'z'}, dimensions={0} | all-to-all | bytes 16384 | tf_op jit(solution)/shard_map/all_to_all | solution.py:392
  96.9 1.2 %shard_map.72 = (f32[2,64,512]{2,1,0:T(8,128)}, f32[2,64,512]{2,1,0:T(8,128)}) custom-call(f32[16,1,128]{2,1,0:T(1,128)S(1)} %all_to_all.23.got_ref, f32[2,64,512]{2,1,0:T(8,128)S(1)} %get-tuple-element.10.t0, f32[2,64,512]{2,1,0:T(8,128)S(1)} %get-tuple-element.11.t1, f32[2,64,512]{2,1,0:T(8,128)S(1)} %get-tuple-element.12.t2, ...), custom_call_target="tpu_custom_call" | custom-call | tf_op jit(solution)/shard_map/pallas_call | solution.py:393
  (1 shorter events, 0.0 us)
Async XLA Ops:
  0.6 0.7 copy-start.3
  1.3 0.7 copy-start.4
  2.2 39.3 %copy-start.1 = (f32[64,128]{1,0:T(8,128)S(1)}, f32[64,128]{1,0:T(8,128)}, u32[]{:S(2)}) copy-start(f32[64,128]{1,0:T(8,128)} %phi_y_ref.3) | copy-start | bytes 98308
  2.2 39.3 %copy-start.2 = (f32[128,128]{1,0:T(8,128)S(1)}, f32[128,128]{1,0:T(8,128)}, u32[]{:S(2)}) copy-start(f32[128,128]{1,0:T(8,128)} %phi_z_ref.1) | copy-start | bytes 196612
  57.4 6.8 %copy-start = (f32[512,128]{1,0:T(8,128)S(1)}, f32[512,128]{1,0:T(8,128)}, u32[]{:S(2)}) copy-start(f32[512,128]{1,0:T(8,128)} %phi_x_ref.1) | copy-start | bytes 786436

commit v3 on v2

--- a/solution.py
+++ b/solution.py
@@ -120,7 +120,7 @@
 def solve_kernel(
     all_ref, phi_y_ref, phi_x_ref,
     t0_out, t1_out, t2_out, t3_out, t4_out, diag_out, gram_out,
-    rec, fx, fy, fz, dinv, t0, t1, t2, t3, phi_xt,
+    rec, fx, fy, fz, dinv, t0, t1, t2, t3, row_modes,
 ):
     x, c = lax.axis_index("x"), lax.axis_index("c")
     n = 2 * x + c
@@ -163,15 +163,21 @@
                 [jnp.where(second == 0, spread, 0.0), jnp.where(second == 1, spread, 0.0)], axis=0
             ).astype(BF16)
         )
-    for part in range(2):
-        phi_xt[part] = split2(phi_x_ref[...].T)[part]
-    for pair in range(PLANES // 2):
-        block = all_ref[:, 8 * pair : 8 * pair + 8, :].reshape(256, 128)
-        rows = dot3(tuple(lift), split2(block))
-        for half in range(2):
-            log_field = dot3(split2(rows[half * ROWS : (half + 1) * ROWS]), (phi_xt[0], phi_xt[1]))
-            plane = 2 * pair + half
-            rec[plane] = jnp.exp(-(log_field + trend[:, plane : plane + 1]))
+    pairs = PLANES // 2
+    blocks_in = [all_ref[:, 8 * pair : 8 * pair + 8, :].reshape(256, 128) for pair in range(pairs)]
+    rows = dot3(tuple(lift), split2(jnp.concatenate(blocks_in, axis=1)))
+    for pair in range(pairs):
+        for part, half in enumerate(split2(rows[:, 128 * pair : 128 * pair + 128])):
+            row_modes[part, 2 * ROWS * pair : 2 * ROWS * (pair + 1), :] = half
+
+    high_x, low_x = split2(phi_x_ref[...].T)
+    all_x = jnp.concatenate([high_x, high_x, low_x], axis=0)
+    for plane in range(0, PLANES, 3):
+        at = slice(plane * ROWS, (plane + 3) * ROWS)
+        high, low = row_modes[0, at, :], row_modes[1, at, :]
+        log_field = mm(jnp.concatenate([high, low, high], axis=1), all_x)
+        for k in range(3):
+            rec[plane + k] = jnp.exp(-(log_field[k * ROWS : k * ROWS + ROWS] + trend[:, plane + k : plane + k + 1]))
 
     blocks = ROWS // 8
     sub = iota((8, NX), 0)
@@ -180,99 +186,96 @@
         return ref[plane, 8 * block : 8 * block + 8, :]
 
     def ahead(now, following):
-        return jnp.where(sub == 7, pltpu.roll(following, 7, 0), pltpu.roll(now, 7, 0))
+        return pltpu.roll(jnp.where(sub == 0, following, now), 7, 0)
 
     def behind(now, previous):
-        return jnp.where(sub == 0, pltpu.roll(previous, 1, 0), pltpu.roll(now, 1, 0))
+        return pltpu.roll(jnp.where(sub == 7, previous, now), 1, 0)
 
     def inverse(a):
         return pl.reciprocal(a, approx=False)
 
-    for block in range(blocks):
-        fz[0, 8 * block : 8 * block + 8, :] = 2.0 * inverse(rows_of(rec, 0, block) + rows_of(rec, 1, block))
-
-    def faces(plane, carry):
+    def needed(plane, reach):
+        steps = max(DEPTH - plane, plane - DEPTH - 1, 0)
+        return range(1, blocks - 1) if steps == reach else range(blocks)
+
+    for block in range(1, blocks - 1):
+        fz[0, 8 * block : 8 * block + 8, :] = inverse(rows_of(rec, 0, block) + rows_of(rec, 1, block))
+    for plane in range(1, PLANES - 1):
+        full = needed(plane, ITERS)
         last_y = None
         now = rows_of(rec, plane, 0)
-        for block in range(blocks):
+        for block in range(full[-1] + 1):
             at = slice(8 * block, 8 * block + 8)
             following = rows_of(rec, plane, min(block + 1, blocks - 1))
-            face_x = 2.0 * inverse(now + roll_x(now, -1))
-            face_y = 2.0 * inverse(now + ahead(now, following))
-            face_z = 2.0 * inverse(now + rec[plane + 1, at, :])
-            fx[plane, at, :] = face_x
+            face_y = inverse(now + ahead(now, following))
+            if block in full:
+                face_x = inverse(now + roll_x(now, -1))
+                face_z = inverse(now + rec[plane + 1, at, :])
+                fx[plane, at, :] = face_x
+                fz[plane, at, :] = face_z
+                back_x = roll_x(face_x, 1)
+                back_y = behind(face_y, face_y if last_y is None else last_y)
+                below = fz[plane - 1, at, :]
+                if plane == 2 and block not in needed(1, ITERS):
+                    below = inverse(now + rec[plane - 1, at, :])
+                    fz[plane - 1, at, :] = below
+                inv = inverse(face_z + below + face_y + back_y + face_x + back_x)
+                dinv[plane, at, :] = inv + inv
+                t0[plane, at, :] = (face_x - back_x) * inv
             fy[plane, at, :] = face_y
-            fz[plane, at, :] = face_z
-            back_x = roll_x(face_x, 1)
-            back_y = behind(face_y, face_y if last_y is None else last_y)
-            diagonal = face_z + fz[plane - 1, at, :] + face_y + back_y + face_x + back_x
-            inv = inverse(diagonal)
-            dinv[plane, at, :] = inv
-            t0[plane, at, :] = (face_x - back_x) * inv
             last_y = face_y
             now = following
-        return carry
-
-    lax.fori_loop(1, PLANES - 1, faces, 0)
-
-    def neighbours(field, plane, block, now, previous, following, last_flux):
-        at = slice(8 * block, 8 * block + 8)
-        face_x = fx[plane, at, :]
-        face_y = fy[plane, at, :]
-        flux_y = face_y * now
-        total = face_x * roll_x(now, -1) + roll_x(face_x * now, 1)
-        total = total + face_y * ahead(now, following)
-        total = total + behind(flux_y, flux_y if last_flux is None else last_flux)
-        total = total + fz[plane, at, :] * field[plane + 1, at, :]
-        total = total + fz[plane - 1, at, :] * field[plane - 1, at, :]
-        return total * dinv[plane, at, :], flux_y
-
-    def sweep(field, older, target, first, last):
-        def one(plane, carry):
-            flux = None
-            now = rows_of(field, plane, 0)
-            for block in range(blocks):
-                at = slice(8 * block, 8 * block + 8)
-                following = rows_of(field, plane, min(block + 1, blocks - 1))
-                value, flux = neighbours(field, plane, block, now, None, following, flux)
-                if older is not None:
-                    value = 2.0 * value - older[plane, at, :]
-                target[plane, at, :] = value
-                now = following
-            return carry
-
-        lax.fori_loop(first, last, one, 0)
-
-    sweep(t0, None, t1, 2, PLANES - 2)
-    sweep(t1, t0, t2, 3, PLANES - 3)
-    sweep(t2, t1, t3, 4, PLANES - 4)
-
-    def own(index, sums):
-        plane = DEPTH + index
-        sums = list(sums)
-        before = rows_of(t3, plane, 0)
-        flux = rows_of(fy, plane, 0) * before
-        now = rows_of(t3, plane, 1)
-        for block in range(1, blocks - 1):
+
+    def sweep(field, plane, full, emit):
+        flux = None
+        now = rows_of(field, plane, full[0] - 1 if full[0] else 0)
+        for block in range(full[0] - 1 if full[0] else 0, full[-1] + 1):
             at = slice(8 * block, 8 * block + 8)
+            face_y = fy[plane, at, :]
+            flux_y = face_y * now
+            following = rows_of(field, plane, min(block + 1, blocks - 1))
+            if block in full:
+                face_x = fx[plane, at, :]
+                total = face_x * roll_x(now, -1) + roll_x(face_x * now, 1)
+                total = total + face_y * ahead(now, following)
+                total = total + behind(flux_y, flux_y if flux is None else flux)
+                total = total + fz[plane, at, :] * field[plane + 1, at, :]
+                total = total + fz[plane - 1, at, :] * field[plane - 1, at, :]
+                emit(block, at, now, total * dinv[plane, at, :])
+            flux = flux_y
+            now = following
+
+    chain = [t0, t1, t2, t3]
+    for degree in range(1, ITERS):
+        for plane in range(degree + 1, PLANES - degree - 1):
+
+            def keep(block, at, now, value):
+                if degree > 1:
+                    value = value - chain[degree - 2][plane, at, :]
+                chain[degree][plane, at, :] = value
+
+            sweep(chain[degree - 1], plane, needed(plane, ITERS - degree), keep)
+
+    sums = [jnp.zeros((8, 128), F32) for _ in GRAM]
+    for index in range(2):
+
+        def close(block, at, now, value):
+            plane = DEPTH + index
             to = slice(8 * block - 8, 8 * block)
-            following = rows_of(t3, plane, block + 1)
-            value, flux = neighbours(t3, plane, block, now, None, following, flux)
             basis = [t0[plane, at, :], t1[plane, at, :], t2[plane, at, :], now]
-            basis.append(2.0 * value - basis[2])
+            basis.append(value - basis[2])
             diagonal = inverse(dinv[plane, at, :])
             for ref, field in zip((t0_out, t1_out, t2_out, t3_out, t4_out), basis):
                 ref[index, to, :] = field
-            diag_out[index, to, :] = diagonal
+            diag_out[index, to, :] = 4.0 * diagonal
             weighted = [diagonal * field for field in basis[:ITERS]]
             for at_sum, (i, k) in enumerate(GRAM):
                 product = weighted[i] * basis[k]
                 product = (product[:, 0:128] + product[:, 128:256]) + (product[:, 256:384] + product[:, 384:512])
                 sums[at_sum] = sums[at_sum] + product
-            now = following
-        return tuple(sums)
-
-    sums = lax.fori_loop(0, 2, own, tuple(jnp.zeros((8, 128), F32) for _ in GRAM))
+
+        sweep(t3, DEPTH + index, range(1, blocks - 1), close)
+
     lane = iota((1, 128), 1)
     gram = jnp.zeros((1, 128), F32)
     for at_sum, value in enumerate(sums):
@@ -304,19 +307,25 @@
     def shifted(a):
         return [
             0.5 * a[1],
-            a[0] + 0.5 * a[2],
+            0.5 * (a[0] + a[2]),
             0.5 * (a[1] + a[3]),
             0.5 * (a[2] + a[4]),
             0.5 * a[3],
         ]
 
+    def added(terms):
+        while len(terms) > 1:
+            terms = [sum(terms[i : i + 2][1:], terms[i]) for i in range(0, len(terms), 2)]
+        return terms[0]
+
     def paired(a, b):
-        result = zero
-        for i in range(ITERS + 1):
-            for k in range(ITERS + 1):
-                if (i, k) in gram and a[i] is not zero and b[k] is not zero:
-                    result = result + a[i] * gram[i, k] * b[k]
-        return result
+        return added(
+            [
+                a[i] * added([gram[i, k] * b[k] for k in range(ITERS + 1) if (i, k) in gram and b[k] is not zero])
+                for i in range(ITERS + 1)
+                if a[i] is not zero
+            ]
+        )
 
     scaled = [jnp.ones((8, 128), F32)] + [zero] * ITERS
     direction = list(scaled)
@@ -384,7 +393,7 @@
         solve_kernel,
         3,
         [own] * 6 + [array(32, 1, 128)],
-        [field] * 9 + [pltpu.VMEM((2, 128, NX), BF16)],
+        [field] * 9 + [pltpu.VMEM((2, PLANES * ROWS, 128), BF16)],
         32,
     )(parcels, phi_y, phi_x)
     gram = lax.all_to_all(gram, ("y", "x", "c"), 0, 0, tiled=True)

time: 98.4 us -> 94.9 us (0.964)
  Pallas kernels: 10.3 us -> 6.76 us
    pallas_call x1, Pallas kernels: 8.12 us -> 4.64 us  [local(): call(solve_kernel, 3, [own] * 6 + [array(32, 1, 128)], [field] * 9 + [plt...]
where the time goes in v3:
time: 94.9 us; the launch traced here: 94.5 us
  blocking collectives  85.7 us (90%)
  Pallas kernels  6.76 us (7%)
  local copies, waits for them, and re-layouts  1.41 us (1%)
    all_to_all x1, blocking collectives, local(): got = lax.all_to_all(packed, ('y', 'z'), 0, 0, tiled=True).reshape(576, 128)  39.2 us
    all_to_all x1, blocking collectives, local(): parcels = lax.all_to_all(parcels, ('y', 'x'), 0, 0, tiled=True)  15.1 us
    all_to_all x1, blocking collectives, local(): gram = lax.all_to_all(gram, 'z', 0, 0, tiled=True)  14.2 us
    all_to_all x1, blocking collectives, local(): gram = lax.all_to_all(gram, ('y', 'x', 'c'), 0, 0, tiled=True)  10.3 us
    all_gather x1, blocking collectives, local(): parcels = lax.all_gather(parcels, 'c', tiled=True)  6.83 us
    pallas_call x1, Pallas kernels, local(): call(solve_kernel, 3, [own] * 6 + [array(32, 1, 128)], [field] * 9 + [plt...  4.64 us

profile of v3, /device:TPU:1, one launch (start us, length us, event | category | flops | bytes accessed | tf_op | source)
XLA Modules:
  0.0 94.5 jit_solution(13216481804449990906)
XLA Ops:
  0.6 0.0 copy-start.3
  0.6 0.7 copy-done.3
  1.3 0.0 copy-start.4
  1.4 0.7 copy-done.4
  2.0 0.2 shard_map.68
  2.2 0.0 copy-start.1
  2.2 0.0 copy-start.2
  2.2 39.2 %all_to_all.20 = f32[576,1,128]{2,1,0:T(1,128)S(1)} all-to-all(f32[576,1,128]{2,1,0:T(1,128)S(1)} %shard_map.68), channel_id=1, replica_groups=mesh['y'=4,'z'=16,'x'=4,'c'=2] {'y','z'}, dimensions={0} | all-to-all | bytes 589824 | tf_op jit(solution)/shard_map/all_to_all | solution.py:386
  41.4 0.0 copy-done.1
  41.5 0.0 copy-done.2
  41.5 0.8 shard_map.69
  42.3 15.1 %all_to_all.21 = f32[16,56,128]{2,1,0:T(8,128)S(1)} all-to-all(f32[16,56,128]{2,1,0:T(8,128)S(1)} %shard_map.69), channel_id=1, replica_groups=mesh['y'=4,'z'=16,'x'=4,'c'=2] {'y','x'}, dimensions={0} | all-to-all | bytes 917504 | tf_op jit(solution)/shard_map/all_to_all | solution.py:388
  57.4 0.0 copy-start
  57.4 6.8 %all_gather.3.all_ref = f32[32,56,128]{2,1,0:T(8,128)S(1)} all-gather(f32[16,56,128]{2,1,0:T(8,128)S(1)} %all_to_all.21), channel_id=1, replica_groups=mesh['y'=4,'z'=16,'x'=4,'c'=2] {'c'}, dimensions={0}, use_global_device_ids=true | all-gather | bytes 1376256 | tf_op jit(solution)/shard_map/all_gather | solution.py:389
  64.2 0.0 copy-done
  64.2 4.6 %shard_map.70 = (f32[2,64,512]{2,1,0:T(8,128)S(1)}, f32[2,64,512]{2,1,0:T(8,128)S(1)}, f32[2,64,512]{2,1,0:T(8,128)S(1)}, f32[2,64,512]{2,1,0:T(8,128)S(1)}, f32...) custom-call(f32[32,56,128]{2,1,0:T(8,128)S(1)} %all_gather.3.all_ref, ...), custom_call_target="tpu_custom_call" | custom-call | tf_op jit(solution)/shard_map/pallas_call | solution.py:392
  68.8 10.3 %all_to_all.22.got_ref = f32[32,1,128]{2,1,0:T(1,128)S(1)} all-to-all(f32[32,1,128]{2,1,0:T(1,128)S(1)} %get-tuple-element.9), channel_id=1, replica_groups=mesh['y'=4,'z'=16,'x'=4,'c'=2] {'y','x','c'}, dimensions={0} | all-to-all | bytes 32768 | tf_op jit(solution)/shard_map/all_to_all | solution.py:399
  79.2 14.2 %all_to_all.23.got_ref = f32[16,1,128]{2,1,0:T(1,128)S(1)} all-to-all(f32[16,1,128]{2,1,0:T(1,128)S(1)} %shard_map.71), channel_id=1, replica_groups=mesh['y'=4,'z'=16,'x'=4,'c'=2] {'z'}, dimensions={0} | all-to-all | bytes 16384 | tf_op jit(solution)/shard_map/all_to_all | solution.py:401
  93.4 1.1 %shard_map.72 = (f32[2,64,512]{2,1,0:T(8,128)}, f32[2,64,512]{2,1,0:T(8,128)}) custom-call(f32[16,1,128]{2,1,0:T(1,128)S(1)} %all_to_all.23.got_ref, f32[2,64,512]{2,1,0:T(8,128)S(1)} %get-tuple-element.10.t0, f32[2,64,512]{2,1,0:T(8,128)S(1)} %get-tuple-element.11.t1, f32[2,64,512]{2,1,0:T(8,128)S(1)} %get-tuple-element.12.t2, ...), custom_call_target="tpu_custom_call" | custom-call | tf_op jit(solution)/shard_map/pallas_call | solution.py:402
  (1 shorter events, 0.0 us)
Async XLA Ops:
  0.6 0.7 copy-start.3
  1.3 0.7 copy-start.4
  2.2 39.3 %copy-start.1 = (f32[64,128]{1,0:T(8,128)S(1)}, f32[64,128]{1,0:T(8,128)}, u32[]{:S(2)}) copy-start(f32[64,128]{1,0:T(8,128)} %phi_y_ref.3) | copy-start | bytes 98308
  2.2 39.3 %copy-start.2 = (f32[128,128]{1,0:T(8,128)S(1)}, f32[128,128]{1,0:T(8,128)}, u32[]{:S(2)}) copy-start(f32[128,128]{1,0:T(8,128)} %phi_z_ref.1) | copy-start | bytes 196612
  57.4 6.8 %copy-start = (f32[512,128]{1,0:T(8,128)S(1)}, f32[512,128]{1,0:T(8,128)}, u32[]{:S(2)}) copy-start(f32[512,128]{1,0:T(8,128)} %phi_x_ref.1) | copy-start | bytes 786436

commit v4 on v3

--- a/solution.py
+++ b/solution.py
@@ -13,7 +13,8 @@
 PLANES = 2 + 2 * DEPTH
 ROWS = 80
 NX = 512
-PARCEL = 56
+SENT = 5
+PARCEL = 28
 GRAM = [(i, j) for i in range(ITERS + 1) for j in range(i, ITERS + 1) if i < ITERS]
 BF16 = jnp.bfloat16
 F32 = jnp.float32
@@ -58,59 +59,57 @@
 
 def pack_kernel(coef_ref, trend_ref, out_ref):
     trend = jnp.concatenate([trend_ref[0:1, :], trend_ref[1:2, :]], axis=1)
-    for quarter in range(4):
+    for part in range(8):
         rows = []
         for r in range(2):
-            for jj in range(4):
-                at = 4 * quarter + jj
+            for jj in range(2):
+                at = 2 * part + jj
                 rows.append(coef_ref[r, at : at + 1, :])
         rows.append(trend)
-        for z in range(16):
+        for h in range(8):
+            to = (part >> 1) * 16 + h * 2 + (part & 1)
             for s, row in enumerate(rows):
-                out_ref[(quarter * 16 + z) * 9 + s] = row
+                out_ref[to * SENT + s] = row
 
 
 def planes_kernel(got_ref, phi_z_ref, phi_y_ref, out_ref):
-    y, z = lax.axis_index("y"), lax.axis_index("z")
+    y, h, l = lax.axis_index("y"), lax.axis_index("h"), lax.axis_index("l")
+    mine = 4 * l + y
+    s1 = iota((32, 128), 0)
+    k1 = iota((32, 128), 1)
+    s5 = iota((32, 64 * SENT), 0)
+    row = iota((32, 64 * SENT), 1)
+    source = (row * 13108) >> 16
+    part = row - SENT * source
+    s6 = iota((32, 64), 0)
+    e6 = iota((32, 64), 1)
+    edge = 2 * mine + s6 - 25
+    edge = jnp.where(edge < 8, edge, edge + 48)
+    edge_pick = one_hot((s6 >= 25) & (s6 < 27) & (e6 == edge))
+    same_mode = (part < 4) & ((part & 1) == (s5 & 1)) & (s5 < 24)
     modes = []
-    rest = []
-    edges = []
-    s1 = iota((PARCEL, 128), 0)
-    k1 = iota((PARCEL, 128), 1)
-    s9 = iota((PARCEL, 576), 0)
-    row = iota((PARCEL, 576), 1)
-    source = (row * 7282) >> 16
-    part = row - 9 * source
-    s6 = iota((PARCEL, 64), 0)
-    e6 = iota((PARCEL, 64), 1)
-    edge = 4 * y + s6 - 50
-    edge = jnp.where(edge < 8, edge, edge + 48)
-    edge_pick = one_hot((s6 >= 50) & (s6 < 54) & (e6 == edge))
-    same_mode = (part < 8) & ((part & 3) == (s9 & 3)) & (s9 < 48)
-    for to in range(4):
-        plane = (2 * (16 * to + z) - DEPTH + (s1 >> 2)) & 127
-        modes.append(one_hot((plane == k1) & (s1 < 48)))
-        wide = (16 * to + z - 3 + 2 * y + s9 - 48) & 63
-        rest.append(one_hot((part == 8) & (source == wide) & (s9 >= 48) & (s9 < 50)))
-        edges.append(edge_pick)
-    modes = jnp.concatenate(modes, axis=0)
-    phi = split2(pick_left(modes, phi_z_ref[...]))
-    k2 = iota((128, 576), 0)
-    r2 = iota((128, 576), 1)
-    src2 = (r2 * 7282) >> 16
-    part2 = r2 - 9 * src2
-    spread = one_hot((k2 == 2 * src2 + (part2 >> 2)) & (part2 < 8))
-    keep = jnp.concatenate([same_mode] * 4, axis=0)
-    high = jnp.where(keep, mm(phi[0], spread), 0.0).astype(BF16)
+    trends = []
+    for to in range(8):
+        wide = 16 * (to & 3) + 2 * h + (to >> 2)
+        plane = (2 * wide - DEPTH + (s1 >> 1)) & 127
+        modes.append(one_hot((plane == k1) & (s1 < 24)))
+        trends.append(one_hot((part == 4) & (source == ((wide - 3 + mine) & 63)) & (s5 == 24)))
+    phi = split2(pick_left(jnp.concatenate(modes, axis=0), phi_z_ref[...]))
+    k2 = iota((128, 64 * SENT), 0)
+    r2 = iota((128, 64 * SENT), 1)
+    src2 = (r2 * 13108) >> 16
+    part2 = r2 - SENT * src2
+    spread = one_hot((k2 == 2 * src2 + (part2 >> 1)) & (part2 < 4))
+    keep = jnp.concatenate([same_mode] * 8, axis=0)
+    high = jnp.where(keep, mm(phi[0], spread), 0.0).astype(BF16) + jnp.concatenate(trends, axis=0)
     low = jnp.where(keep, mm(phi[1], spread), 0.0).astype(BF16)
-    high = high + jnp.concatenate(rest, axis=0)
-    got = split2(got_ref[...])
-    result = dot3((high, low), got)
+    result = dot3((high, low), split2(got_ref[...]))
     edge_rows = pick_left(edge_pick, phi_y_ref[...])
-    for to in range(4):
-        block = result[to * PARCEL : (to + 1) * PARCEL] + edge_rows
+    for to in range(8):
+        block = (result[to * 32 : to * 32 + 32] + edge_rows)[0:PARCEL]
         for x in range(4):
-            out_ref[to * 4 + x] = block
+            at = (to * 4 + x) * PARCEL
+            out_ref[at : at + PARCEL, :] = block
 
 
 def roll_x(a, shift):
@@ -125,50 +124,57 @@
     x, c = lax.axis_index("x"), lax.axis_index("c")
     n = 2 * x + c
 
-    tail = all_ref[:, 48:56, :].reshape(256, 128)
+    lower = iota((8, 128), 0) < 4
+
+    def tile(pair, at):
+        start = 2 * PARCEL * pair + 8 * at
+        return all_ref[start : start + 8, :]
+
+    def chunk(at):
+        tiles = []
+        for pair in range(32):
+            tiles.append(tile(pair, at))
+            tiles.append(jnp.where(lower, tile(pair, at + 4), tile(pair, at + 3)))
+        return jnp.concatenate(tiles, axis=0)
+
+    tail = jnp.concatenate([jnp.where(lower, tile(pair, 3), tile(pair, 6)) for pair in range(32)], axis=0)
     h = iota((16, 256), 0)
     col = iota((16, 256), 1)
     edge = jnp.where(h < 8, h + 8, h - 8)
     other = jnp.where(h < 8, n + 7, n + 1) & 7
-    want = (((other & 1) * 16 + (edge >> 2) * 4 + (other >> 1)) * 8) + 2 + (edge & 3)
+    want = ((other & 1) * 32 + (edge >> 1) * 4 + (other >> 1)) * 4 + 1 + (edge & 1)
     halo = pick_left(one_hot(col == want), tail)
     phi_ext = jnp.concatenate([halo[0:8], phi_y_ref[...], halo[8:16]], axis=0)
 
     tail_t = tail.T
     a = iota((256, 48), 0)
     b = iota((256, 48), 1)
-    src, s = a >> 3, a & 7
-    a_n = 2 * (src & 3) + (src >> 4)
-    q = 2 * ((src >> 2) & 3) + s
+    src, s = a >> 2, a & 3
+    a_n = 2 * (src & 3) + (src >> 5)
+    q = (src >> 2) & 7
     p = b & 15
     group = b >> 4
     from_n = jnp.where(group == 0, n, jnp.where(group == 1, n + 7, n + 1)) & 7
-    right = (s < 2) & (a_n == from_n)
+    right = (s == 0) & (a_n == from_n)
     trend = pick_right(tail_t[0:64], one_hot(right & (2 * q == p + 1))) + pick_right(
         tail_t[64:128], one_hot(right & (2 * q + 1 == p + 1))
     )
     trend = jnp.concatenate([trend[56:64, 16:32], trend[:, 0:16], trend[0:8, 32:48]], axis=0)
 
-    j = iota((128, 256), 0)
-    col = iota((128, 256), 1)
+    j = iota((128, 512), 0)
+    col = iota((128, 512), 1)
     src = col >> 3
-    col_j = 16 * (2 * (src & 3) + (src >> 4)) + 4 * ((src >> 2) & 3) + (col & 3)
-    order = one_hot(j == col_j)
-    second = (iota((ROWS, 256), 1) >> 2) & 1
+    order = one_hot(j == 16 * (2 * (src & 3) + (src >> 5)) + 4 * ((src >> 2) & 3) + 2 * ((src >> 4) & 1) + (col & 1))
+    col = iota((ROWS, 512), 1)
+    fourth = ((col >> 1) & 3) ^ (((col >> 3) & 1) << 1)
     lift = []
     for half in split2(phi_ext):
         spread = mm(half, order)
-        lift.append(
-            jnp.concatenate(
-                [jnp.where(second == 0, spread, 0.0), jnp.where(second == 1, spread, 0.0)], axis=0
-            ).astype(BF16)
-        )
-    pairs = PLANES // 2
-    blocks_in = [all_ref[:, 8 * pair : 8 * pair + 8, :].reshape(256, 128) for pair in range(pairs)]
-    rows = dot3(tuple(lift), split2(jnp.concatenate(blocks_in, axis=1)))
-    for pair in range(pairs):
-        for part, half in enumerate(split2(rows[:, 128 * pair : 128 * pair + 128])):
-            row_modes[part, 2 * ROWS * pair : 2 * ROWS * (pair + 1), :] = half
+        lift.append(jnp.concatenate([jnp.where(fourth == k, spread, 0.0) for k in range(4)], axis=0).astype(BF16))
+    rows = dot3(tuple(lift), split2(jnp.concatenate([chunk(at) for at in range(3)], axis=1)))
+    for group in range(3):
+        for part, half in enumerate(split2(rows[:, 128 * group : 128 * group + 128])):
+            row_modes[part, 4 * ROWS * group : 4 * ROWS * (group + 1), :] = half
 
     high_x, low_x = split2(phi_x_ref[...].T)
     all_x = jnp.concatenate([high_x, high_x, low_x], axis=0)
@@ -382,11 +388,12 @@
 
 
 def local(coefficients, phi_x, phi_y, phi_z, log_trend):
-    packed = call(pack_kernel, 2, array(576, 1, 128))(coefficients, log_trend)
-    got = lax.all_to_all(packed, ("y", "z"), 0, 0, tiled=True).reshape(576, 128)
-    parcels = call(planes_kernel, 3, array(16, PARCEL, 128))(got, phi_z, phi_y)
-    parcels = lax.all_to_all(parcels, ("y", "x"), 0, 0, tiled=True)
-    parcels = lax.all_gather(parcels, "c", tiled=True)
+    packed = call(pack_kernel, 2, array(64 * SENT, 1, 128))(coefficients, log_trend)
+    got = lax.all_to_all(packed, ("y", "h", "l"), 0, 0, tiled=True).reshape(64 * SENT, 128)
+    parcels = call(planes_kernel, 3, array(32 * PARCEL, 128))(got, phi_z, phi_y)
+    parcels = parcels.reshape(32 * PARCEL, 1, 128)
+    parcels = lax.all_to_all(parcels, ("l", "y", "x"), 0, 0, tiled=True)
+    parcels = lax.all_gather(parcels.reshape(32 * PARCEL, 128), "c", tiled=True)
     own = array(2, 64, NX)
     field = pltpu.VMEM((PLANES, ROWS, NX), F32)
     *basis, diagonal, gram = call(
@@ -398,13 +405,13 @@
     )(parcels, phi_y, phi_x)
     gram = lax.all_to_all(gram, ("y", "x", "c"), 0, 0, tiled=True)
     gram = call(relay_kernel, 1, array(16, 1, 128))(gram)
-    gram = lax.all_to_all(gram, "z", 0, 0, tiled=True)
+    gram = lax.all_to_all(gram, ("h", "l"), 0, 0, tiled=True)
     return tuple(call(combine_kernel, 7, [own, own])(gram, *basis, diagonal))
 
 
 def solution(mesh):
-    chips = Mesh(mesh.devices.reshape(4, 16, 4, 2), ("y", "z", "x", "c"))
-    wide, narrow = ("y", "z"), ("x", "c")
+    chips = Mesh(mesh.devices.reshape(4, 8, 2, 4, 2), ("y", "h", "l", "x", "c"))
+    wide, narrow = ("y", "h", "l"), ("x", "c")
     return jax.shard_map(
         local,
         mesh=chips,

time: 94.9 us -> 91 us (0.959)
  blocking collectives: 85.7 us -> 81.7 us
    all_to_all x3, blocking collectives: 68.5 us -> 65.7 us  [the longest x1 34.3 us: local(): lax.all_to_all(packed, ('y', 'h', 'l'), 0, 0, tiled=True)]
    all_gather x1, blocking collectives: 6.83 us -> 5.14 us  [local(): parcels = lax.all_gather(parcels.reshape(32 * PARCEL, 128), 'c', tiled=True)]
where the time goes in v4:
time: 91 us; the launch traced here: 90.6 us
  blocking collectives  81.7 us (90%)
  Pallas kernels  6.88 us (8%)
  local copies, waits for them, and re-layouts  1.41 us (2%)
    all_to_all x1, blocking collectives, local(): lax.all_to_all(packed, ('y', 'h', 'l'), 0, 0, tiled=True)  34.3 us
    all_to_all x1, blocking collectives, local(): parcels = lax.all_to_all(parcels, ('l', 'y', 'x'), 0, 0, tiled=True)  17.2 us
    all_to_all x1, blocking collectives, local(): gram = lax.all_to_all(gram, ('h', 'l'), 0, 0, tiled=True)  14.2 us
    all_to_all x1, blocking collectives, local(): gram = lax.all_to_all(gram, ('y', 'x', 'c'), 0, 0, tiled=True)  10.9 us
    all_gather x1, blocking collectives, local(): parcels = lax.all_gather(parcels.reshape(32 * PARCEL, 128), 'c', tiled=True)  5.14 us
    pallas_call x1, Pallas kernels, local(): call(solve_kernel, 3, [own] * 6 + [array(32, 1, 128)], [field] * 9 + [plt...  4.92 us

profile of v4, /device:TPU:1, one launch (start us, length us, event | category | flops | bytes accessed | tf_op | source)
XLA Modules:
  0.0 90.6 jit_solution(2869279007042531566)
XLA Ops:
  0.6 0.0 copy-start.3
  0.6 0.7 copy-done.3
  1.3 0.0 copy-start.4
  1.4 0.7 copy-done.4
  2.0 0.1 shard_map.68
  2.1 0.0 copy-start.1
  2.1 0.0 copy-start.2
  2.1 34.3 %all_to_all.20 = f32[320,1,128]{2,1,0:T(1,128)S(1)} all-to-all(f32[320,1,128]{2,1,0:T(1,128)S(1)} %shard_map.68), channel_id=1, replica_groups=mesh['y'=4,'h'=8,'l'=2,'x'=4,'c'=2] {'y','h','l'}, dimensions={0} | all-to-all | bytes 327680 | tf_op jit(solution)/shard_map/all_to_all | solution.py:392
  36.4 0.0 copy-done.1
  36.4 0.0 copy-done.2
  36.5 0.7 shard_map.69
  37.2 17.2 %all_to_all.21 = f32[896,1,128]{2,1,0:T(1,128)S(1)} all-to-all(f32[896,1,128]{2,1,0:T(1,128)S(1)} %bitcast.7), channel_id=1, replica_groups=mesh['y'=4,'h'=8,'l'=2,'x'=4,'c'=2] {'l','y','x'}, dimensions={0} | all-to-all | bytes 917504 | tf_op jit(solution)/shard_map/all_to_all | solution.py:395
  54.4 0.0 copy-start
  54.4 5.1 %all-gather = f32[1792,1,128]{2,0,1:T(8,128)S(1)} all-gather(f32[896,1,128]{2,0,1:T(8,128)S(1)} %bitcast.9), channel_id=2, replica_groups=mesh['y'=4,'h'=8,'l'=2,'x'=4,'c'=2] {'c'}, dimensions={0}, use_global_device_ids=true | all-gather | bytes 1376256 | tf_op jit(solution)/shard_map/all_gather | solution.py:396
  59.5 0.0 copy-done
  59.5 4.9 %shard_map.70 = (f32[2,64,512]{2,1,0:T(8,128)S(1)}, f32[2,64,512]{2,1,0:T(8,128)S(1)}, f32[2,64,512]{2,1,0:T(8,128)S(1)}, f32[2,64,512]{2,1,0:T(8,128)S(1)}, f32...) custom-call(f32[1792,128]{1,0:T(8,128)S(1)} %bitcast.6, f32[64,128]{1,0:T(8,128)S(1)} %copy-done.1, ...), custom_call_target="tpu_custom_call" | custom-call | tf_op jit(solution)/shard_map/pallas_call | solution.py:399
  64.5 10.9 %all_to_all.22.got_ref = f32[32,1,128]{2,1,0:T(1,128)S(1)} all-to-all(f32[32,1,128]{2,1,0:T(1,128)S(1)} %get-tuple-element.9), channel_id=1, replica_groups=mesh['y'=4,'h'=8,'l'=2,'x'=4,'c'=2] {'y','x','c'}, dimensions={0} | all-to-all | bytes 32768 | tf_op jit(solution)/shard_map/all_to_all | solution.py:406
  75.4 14.2 %all_to_all.23.got_ref = f32[16,1,128]{2,1,0:T(1,128)S(1)} all-to-all(f32[16,1,128]{2,1,0:T(1,128)S(1)} %shard_map.71), channel_id=1, replica_groups=mesh['y'=4,'h'=8,'l'=2,'x'=4,'c'=2] {'h','l'}, dimensions={0} | all-to-all | bytes 16384 | tf_op jit(solution)/shard_map/all_to_all | solution.py:408
  89.5 1.1 %shard_map.72 = (f32[2,64,512]{2,1,0:T(8,128)}, f32[2,64,512]{2,1,0:T(8,128)}) custom-call(f32[16,1,128]{2,1,0:T(1,128)S(1)} %all_to_all.23.got_ref, f32[2,64,512]{2,1,0:T(8,128)S(1)} %get-tuple-element.10.t0, f32[2,64,512]{2,1,0:T(8,128)S(1)} %get-tuple-element.11.t1, f32[2,64,512]{2,1,0:T(8,128)S(1)} %get-tuple-element.12.t2, ...), custom_call_target="tpu_custom_call" | custom-call | tf_op jit(solution)/shard_map/pallas_call | solution.py:409
  (1 shorter events, 0.0 us)
Async XLA Ops:
  0.6 0.7 copy-start.3
  1.3 0.7 copy-start.4
  2.1 34.3 %copy-start.1 = (f32[64,128]{1,0:T(8,128)S(1)}, f32[64,128]{1,0:T(8,128)}, u32[]{:S(2)}) copy-start(f32[64,128]{1,0:T(8,128)} %phi_y_ref.3) | copy-start | bytes 98308
  2.1 34.3 %copy-start.2 = (f32[128,128]{1,0:T(8,128)S(1)}, f32[128,128]{1,0:T(8,128)}, u32[]{:S(2)}) copy-start(f32[128,128]{1,0:T(8,128)} %phi_z_ref.1) | copy-start | bytes 196612
  54.4 5.1 %copy-start = (f32[512,128]{1,0:T(8,128)S(1)}, f32[512,128]{1,0:T(8,128)}, u32[]{:S(2)}) copy-start(f32[512,128]{1,0:T(8,128)} %phi_x_ref.1) | copy-start | bytes 786436

commit v5 on v4

--- a/solution.py
+++ b/solution.py
@@ -59,17 +59,15 @@
 
 def pack_kernel(coef_ref, trend_ref, out_ref):
     trend = jnp.concatenate([trend_ref[0:1, :], trend_ref[1:2, :]], axis=1)
-    for part in range(8):
-        rows = []
-        for r in range(2):
-            for jj in range(2):
-                at = 2 * part + jj
-                rows.append(coef_ref[r, at : at + 1, :])
-        rows.append(trend)
-        for h in range(8):
-            to = (part >> 1) * 16 + h * 2 + (part & 1)
-            for s, row in enumerate(rows):
-                out_ref[to * SENT + s] = row
+    for y in range(4):
+        pair = []
+        for l in range(2):
+            at = slice(4 * y + 2 * l, 4 * y + 2 * l + 2)
+            pair += [coef_ref[0, at, :], coef_ref[1, at, :], trend]
+        block = jnp.concatenate(pair * 4, axis=0)
+        for half in range(2):
+            start = (2 * y + half) * 8 * SENT
+            out_ref[start : start + 8 * SENT, :] = block
 
 
 def planes_kernel(got_ref, phi_z_ref, phi_y_ref, out_ref):
@@ -108,7 +106,7 @@
     for to in range(8):
         block = (result[to * 32 : to * 32 + 32] + edge_rows)[0:PARCEL]
         for x in range(4):
-            at = (to * 4 + x) * PARCEL
+            at = (x * 8 + to) * PARCEL
             out_ref[at : at + PARCEL, :] = block
 
 
@@ -130,19 +128,12 @@
         start = 2 * PARCEL * pair + 8 * at
         return all_ref[start : start + 8, :]
 
-    def chunk(at):
-        tiles = []
-        for pair in range(32):
-            tiles.append(tile(pair, at))
-            tiles.append(jnp.where(lower, tile(pair, at + 4), tile(pair, at + 3)))
-        return jnp.concatenate(tiles, axis=0)
-
     tail = jnp.concatenate([jnp.where(lower, tile(pair, 3), tile(pair, 6)) for pair in range(32)], axis=0)
     h = iota((16, 256), 0)
     col = iota((16, 256), 1)
     edge = jnp.where(h < 8, h + 8, h - 8)
     other = jnp.where(h < 8, n + 7, n + 1) & 7
-    want = ((other & 1) * 32 + (edge >> 1) * 4 + (other >> 1)) * 4 + 1 + (edge & 1)
+    want = ((other & 1) * 32 + (other >> 1) * 8 + (edge >> 1)) * 4 + 1 + (edge & 1)
     halo = pick_left(one_hot(col == want), tail)
     phi_ext = jnp.concatenate([halo[0:8], phi_y_ref[...], halo[8:16]], axis=0)
 
@@ -150,8 +141,8 @@
     a = iota((256, 48), 0)
     b = iota((256, 48), 1)
     src, s = a >> 2, a & 3
-    a_n = 2 * (src & 3) + (src >> 5)
-    q = (src >> 2) & 7
+    a_n = 2 * ((src >> 3) & 3) + (src >> 5)
+    q = src & 7
     p = b & 15
     group = b >> 4
     from_n = jnp.where(group == 0, n, jnp.where(group == 1, n + 7, n + 1)) & 7
@@ -161,20 +152,19 @@
     )
     trend = jnp.concatenate([trend[56:64, 16:32], trend[:, 0:16], trend[0:8, 32:48]], axis=0)
 
-    j = iota((128, 512), 0)
-    col = iota((128, 512), 1)
-    src = col >> 3
-    order = one_hot(j == 16 * (2 * (src & 3) + (src >> 5)) + 4 * ((src >> 2) & 3) + 2 * ((src >> 4) & 1) + (col & 1))
-    col = iota((ROWS, 512), 1)
-    fourth = ((col >> 1) & 3) ^ (((col >> 3) & 1) << 1)
-    lift = []
-    for half in split2(phi_ext):
-        spread = mm(half, order)
-        lift.append(jnp.concatenate([jnp.where(fourth == k, spread, 0.0) for k in range(4)], axis=0).astype(BF16))
-    rows = dot3(tuple(lift), split2(jnp.concatenate([chunk(at) for at in range(3)], axis=1)))
-    for group in range(3):
-        for part, half in enumerate(split2(rows[:, 128 * group : 128 * group + 128])):
-            row_modes[part, 4 * ROWS * group : 4 * ROWS * (group + 1), :] = half
+    j = iota((128, 128), 0)
+    col = iota((128, 128), 1)
+    src, jj = col & 63, col >> 6
+    order = one_hot(j == 16 * (2 * ((src >> 3) & 3) + (src >> 5)) + 4 * (src & 3) + 2 * ((src >> 2) & 1) + jj)
+    lift = tuple(mm(half, order).astype(BF16) for half in split2(phi_ext))
+    modes = [
+        jnp.concatenate([all_ref[pl.ds(2 * plane + jj, 64, stride=PARCEL), :] for jj in range(2)], axis=0)
+        for plane in range(PLANES)
+    ]
+    rows = dot3(lift, split2(jnp.concatenate(modes, axis=1)))
+    for plane in range(PLANES):
+        for part, half in enumerate(split2(rows[:, 128 * plane : 128 * plane + 128])):
+            row_modes[part, ROWS * plane : ROWS * (plane + 1), :] = half
 
     high_x, low_x = split2(phi_x_ref[...].T)
     all_x = jnp.concatenate([high_x, high_x, low_x], axis=0)
@@ -388,11 +378,11 @@
 
 
 def local(coefficients, phi_x, phi_y, phi_z, log_trend):
-    packed = call(pack_kernel, 2, array(64 * SENT, 1, 128))(coefficients, log_trend)
+    packed = call(pack_kernel, 2, array(64 * SENT, 128))(coefficients, log_trend).reshape(64 * SENT, 1, 128)
     got = lax.all_to_all(packed, ("y", "h", "l"), 0, 0, tiled=True).reshape(64 * SENT, 128)
     parcels = call(planes_kernel, 3, array(32 * PARCEL, 128))(got, phi_z, phi_y)
     parcels = parcels.reshape(32 * PARCEL, 1, 128)
-    parcels = lax.all_to_all(parcels, ("l", "y", "x"), 0, 0, tiled=True)
+    parcels = lax.all_to_all(parcels, ("x", "l", "y"), 0, 0, tiled=True)
     parcels = lax.all_gather(parcels.reshape(32 * PARCEL, 128), "c", tiled=True)
     own = array(2, 64, NX)
     field = pltpu.VMEM((PLANES, ROWS, NX), F32)

time: 91 us -> 90.4 us (level)
  no operation moved by 1% of the time
where the time goes in v5:
time: 90.4 us; the launch traced here: 90 us
  blocking collectives  81.4 us (90%)
  Pallas kernels  6.52 us (7%)
  local copies, waits for them, and re-layouts  1.41 us (2%)
    all_to_all x1, blocking collectives, local(): lax.all_to_all(packed, ('y', 'h', 'l'), 0, 0, tiled=True)  34.3 us
    all_to_all x1, blocking collectives, local(): parcels = lax.all_to_all(parcels, ('x', 'l', 'y'), 0, 0, tiled=True)  17.2 us
    all_to_all x1, blocking collectives, local(): gram = lax.all_to_all(gram, ('h', 'l'), 0, 0, tiled=True)  14.2 us
    all_to_all x1, blocking collectives, local(): gram = lax.all_to_all(gram, ('y', 'x', 'c'), 0, 0, tiled=True)  10.6 us
    all_gather x1, blocking collectives, local(): parcels = lax.all_gather(parcels.reshape(32 * PARCEL, 128), 'c', tiled=True)  5.23 us
    pallas_call x1, Pallas kernels, local(): call(solve_kernel, 3, [own] * 6 + [array(32, 1, 128)], [field] * 9 + [plt...  4.57 us

profile of v5, /device:TPU:1, one launch (start us, length us, event | category | flops | bytes accessed | tf_op | source)
XLA Modules:
  0.0 90.0 jit_solution(1646523416232669938)
XLA Ops:
  0.6 0.0 copy-start.3
  0.6 0.7 copy-done.3
  1.3 0.0 copy-start.4
  1.4 0.7 copy-done.4
  2.0 0.1 shard_map.68
  2.1 0.0 copy-start.1
  2.1 0.0 copy-start.2
  2.1 34.3 %all_to_all.20 = f32[320,1,128]{2,1,0:T(1,128)S(1)} all-to-all(f32[320,1,128]{2,1,0:T(1,128)S(1)} %bitcast.11), channel_id=1, replica_groups=mesh['y'=4,'h'=8,'l'=2,'x'=4,'c'=2] {'y','h','l'}, dimensions={0} | all-to-all | bytes 327680 | tf_op jit(solution)/shard_map/all_to_all | solution.py:382
  36.4 0.0 copy-done.1
  36.4 0.0 copy-done.2
  36.5 0.7 shard_map.69
  37.2 17.2 %all_to_all.21 = f32[896,1,128]{2,1,0:T(1,128)S(1)} all-to-all(f32[896,1,128]{2,1,0:T(1,128)S(1)} %bitcast.10), channel_id=1, replica_groups=mesh['y'=4,'h'=8,'l'=2,'x'=4,'c'=2] {'x','l','y'}, dimensions={0} | all-to-all | bytes 917504 | tf_op jit(solution)/shard_map/all_to_all | solution.py:385
  54.3 0.0 copy-start
  54.3 5.2 %all-gather = f32[1792,1,128]{2,0,1:T(8,128)S(1)} all-gather(f32[896,1,128]{2,0,1:T(8,128)S(1)} %bitcast.13), channel_id=2, replica_groups=mesh['y'=4,'h'=8,'l'=2,'x'=4,'c'=2] {'c'}, dimensions={0}, use_global_device_ids=true | all-gather | bytes 1376256 | tf_op jit(solution)/shard_map/all_gather | solution.py:386
  59.6 0.0 copy-done
  59.6 4.6 %shard_map.70 = (f32[2,64,512]{2,1,0:T(8,128)S(1)}, f32[2,64,512]{2,1,0:T(8,128)S(1)}, f32[2,64,512]{2,1,0:T(8,128)S(1)}, f32[2,64,512]{2,1,0:T(8,128)S(1)}, f32...) custom-call(f32[1792,128]{1,0:T(8,128)S(1)} %bitcast.9, f32[64,128]{1,0:T(8,128)S(1)} %copy-done.1, ...), custom_call_target="tpu_custom_call" | custom-call | tf_op jit(solution)/shard_map/pallas_call | solution.py:389
  64.1 10.6 %all_to_all.22.got_ref = f32[32,1,128]{2,1,0:T(1,128)S(1)} all-to-all(f32[32,1,128]{2,1,0:T(1,128)S(1)} %get-tuple-element.9), channel_id=1, replica_groups=mesh['y'=4,'h'=8,'l'=2,'x'=4,'c'=2] {'y','x','c'}, dimensions={0} | all-to-all | bytes 32768 | tf_op jit(solution)/shard_map/all_to_all | solution.py:396
  74.8 14.2 %all_to_all.23.got_ref = f32[16,1,128]{2,1,0:T(1,128)S(1)} all-to-all(f32[16,1,128]{2,1,0:T(1,128)S(1)} %shard_map.71), channel_id=1, replica_groups=mesh['y'=4,'h'=8,'l'=2,'x'=4,'c'=2] {'h','l'}, dimensions={0} | all-to-all | bytes 16384 | tf_op jit(solution)/shard_map/all_to_all | solution.py:398
  88.9 1.1 %shard_map.72 = (f32[2,64,512]{2,1,0:T(8,128)}, f32[2,64,512]{2,1,0:T(8,128)}) custom-call(f32[16,1,128]{2,1,0:T(1,128)S(1)} %all_to_all.23.got_ref, f32[2,64,512]{2,1,0:T(8,128)S(1)} %get-tuple-element.10.t0, f32[2,64,512]{2,1,0:T(8,128)S(1)} %get-tuple-element.11.t1, f32[2,64,512]{2,1,0:T(8,128)S(1)} %get-tuple-element.12.t2, ...), custom_call_target="tpu_custom_call" | custom-call | tf_op jit(solution)/shard_map/pallas_call | solution.py:399
  (1 shorter events, 0.0 us)
Async XLA Ops:
  0.6 0.7 copy-start.3
  1.3 0.7 copy-start.4
  2.1 34.3 %copy-start.1 = (f32[64,128]{1,0:T(8,128)S(1)}, f32[64,128]{1,0:T(8,128)}, u32[]{:S(2)}) copy-start(f32[64,128]{1,0:T(8,128)} %phi_y_ref.3) | copy-start | bytes 98308
  2.1 34.3 %copy-start.2 = (f32[128,128]{1,0:T(8,128)S(1)}, f32[128,128]{1,0:T(8,128)}, u32[]{:S(2)}) copy-start(f32[128,128]{1,0:T(8,128)} %phi_z_ref.1) | copy-start | bytes 196612
  54.3 5.2 %copy-start = (f32[512,128]{1,0:T(8,128)S(1)}, f32[512,128]{1,0:T(8,128)}, u32[]{:S(2)}) copy-start(f32[512,128]{1,0:T(8,128)} %phi_x_ref.1) | copy-start | bytes 786436

commit v6 on v5

--- a/solution.py
+++ b/solution.py
@@ -57,7 +57,59 @@
     return jnp.where(condition, 1.0, 0.0).astype(BF16)
 
 
-def pack_kernel(coef_ref, trend_ref, out_ref):
+def choices_kernel(modes, spread, keep, trends, edge_pick, order, halo_pick, trend_pick):
+    y, h, l = lax.axis_index("y"), lax.axis_index("h"), lax.axis_index("l")
+    n = 2 * lax.axis_index("x") + lax.axis_index("c")
+    mine = 4 * l + y
+
+    s1 = iota((32, 128), 0)
+    k1 = iota((32, 128), 1)
+    s5 = iota((32, 64 * SENT), 0)
+    row = iota((32, 64 * SENT), 1)
+    source = (row * 13108) >> 16
+    part = row - SENT * source
+    same_mode = one_hot((part < 4) & ((part & 1) == (s5 & 1)) & (s5 < 24))
+    trend_row = (part == 4) & (s5 == 24)
+    for to in range(8):
+        at = slice(32 * to, 32 * to + 32)
+        wide = 16 * (to & 3) + 2 * h + (to >> 2)
+        plane = (2 * wide - DEPTH + (s1 >> 1)) & 127
+        modes[at, :] = one_hot((plane == k1) & (s1 < 24))
+        keep[at, :] = same_mode
+        trends[at, :] = one_hot(trend_row & (source == ((wide - 3 + mine) & 63)))
+    k2 = iota((128, 64 * SENT), 0)
+    r2 = iota((128, 64 * SENT), 1)
+    source = (r2 * 13108) >> 16
+    part = r2 - SENT * source
+    spread[...] = one_hot((k2 == 2 * source + (part >> 1)) & (part < 4))
+    s6 = iota((32, 64), 0)
+    e6 = iota((32, 64), 1)
+    edge = 2 * mine + s6 - 25
+    edge = jnp.where(edge < 8, edge, edge + 48)
+    edge_pick[...] = one_hot((s6 >= 25) & (s6 < 27) & (e6 == edge))
+
+    row = iota((16, 256), 0)
+    col = iota((16, 256), 1)
+    edge = jnp.where(row < 8, row + 8, row - 8)
+    other = jnp.where(row < 8, n + 7, n + 1) & 7
+    halo_pick[...] = one_hot(col == ((other & 1) * 32 + (other >> 1) * 8 + (edge >> 1)) * 4 + 1 + (edge & 1))
+    a = iota((256, 48), 0)
+    b = iota((256, 48), 1)
+    src, s = a >> 2, a & 3
+    a_n = 2 * ((src >> 3) & 3) + (src >> 5)
+    p = b & 15
+    group = b >> 4
+    from_n = jnp.where(group == 0, n, jnp.where(group == 1, n + 7, n + 1)) & 7
+    right = (s == 0) & (a_n == from_n)
+    for r in range(2):
+        trend_pick[r] = one_hot(right & (2 * (src & 7) + r == p + 1))
+    j = iota((128, 128), 0)
+    col = iota((128, 128), 1)
+    src, jj = col & 63, col >> 6
+    order[...] = one_hot(j == 16 * (2 * ((src >> 3) & 3) + (src >> 5)) + 4 * (src & 3) + 2 * ((src >> 2) & 1) + jj)
+
+
+def pack_kernel(after_ref, coef_ref, trend_ref, out_ref):
     trend = jnp.concatenate([trend_ref[0:1, :], trend_ref[1:2, :]], axis=1)
     for y in range(4):
         pair = []
@@ -70,39 +122,13 @@
             out_ref[start : start + 8 * SENT, :] = block
 
 
-def planes_kernel(got_ref, phi_z_ref, phi_y_ref, out_ref):
-    y, h, l = lax.axis_index("y"), lax.axis_index("h"), lax.axis_index("l")
-    mine = 4 * l + y
-    s1 = iota((32, 128), 0)
-    k1 = iota((32, 128), 1)
-    s5 = iota((32, 64 * SENT), 0)
-    row = iota((32, 64 * SENT), 1)
-    source = (row * 13108) >> 16
-    part = row - SENT * source
-    s6 = iota((32, 64), 0)
-    e6 = iota((32, 64), 1)
-    edge = 2 * mine + s6 - 25
-    edge = jnp.where(edge < 8, edge, edge + 48)
-    edge_pick = one_hot((s6 >= 25) & (s6 < 27) & (e6 == edge))
-    same_mode = (part < 4) & ((part & 1) == (s5 & 1)) & (s5 < 24)
-    modes = []
-    trends = []
-    for to in range(8):
-        wide = 16 * (to & 3) + 2 * h + (to >> 2)
-        plane = (2 * wide - DEPTH + (s1 >> 1)) & 127
-        modes.append(one_hot((plane == k1) & (s1 < 24)))
-        trends.append(one_hot((part == 4) & (source == ((wide - 3 + mine) & 63)) & (s5 == 24)))
-    phi = split2(pick_left(jnp.concatenate(modes, axis=0), phi_z_ref[...]))
-    k2 = iota((128, 64 * SENT), 0)
-    r2 = iota((128, 64 * SENT), 1)
-    src2 = (r2 * 13108) >> 16
-    part2 = r2 - SENT * src2
-    spread = one_hot((k2 == 2 * src2 + (part2 >> 1)) & (part2 < 4))
-    keep = jnp.concatenate([same_mode] * 8, axis=0)
-    high = jnp.where(keep, mm(phi[0], spread), 0.0).astype(BF16) + jnp.concatenate(trends, axis=0)
-    low = jnp.where(keep, mm(phi[1], spread), 0.0).astype(BF16)
+def planes_kernel(got_ref, phi_z_ref, phi_y_ref, modes, spread, keep, trends, edge_pick, out_ref):
+    phi = split2(pick_left(modes[...], phi_z_ref[...]))
+    kept = keep[...].astype(F32)
+    high = (mm(phi[0], spread[...]) * kept).astype(BF16) + trends[...]
+    low = (mm(phi[1], spread[...]) * kept).astype(BF16)
     result = dot3((high, low), split2(got_ref[...]))
-    edge_rows = pick_left(edge_pick, phi_y_ref[...])
+    edge_rows = pick_left(edge_pick[...], phi_y_ref[...])
     for to in range(8):
         block = (result[to * 32 : to * 32 + 32] + edge_rows)[0:PARCEL]
         for x in range(4):
@@ -115,13 +141,10 @@
 
 
 def solve_kernel(
-    all_ref, phi_y_ref, phi_x_ref,
+    all_ref, phi_y_ref, phi_x_ref, order_ref, halo_pick, trend_pick,
     t0_out, t1_out, t2_out, t3_out, t4_out, diag_out, gram_out,
     rec, fx, fy, fz, dinv, t0, t1, t2, t3, row_modes,
 ):
-    x, c = lax.axis_index("x"), lax.axis_index("c")
-    n = 2 * x + c
-
     lower = iota((8, 128), 0) < 4
 
     def tile(pair, at):
@@ -129,34 +152,14 @@
         return all_ref[start : start + 8, :]
 
     tail = jnp.concatenate([jnp.where(lower, tile(pair, 3), tile(pair, 6)) for pair in range(32)], axis=0)
-    h = iota((16, 256), 0)
-    col = iota((16, 256), 1)
-    edge = jnp.where(h < 8, h + 8, h - 8)
-    other = jnp.where(h < 8, n + 7, n + 1) & 7
-    want = ((other & 1) * 32 + (other >> 1) * 8 + (edge >> 1)) * 4 + 1 + (edge & 1)
-    halo = pick_left(one_hot(col == want), tail)
+    halo = pick_left(halo_pick[...], tail)
     phi_ext = jnp.concatenate([halo[0:8], phi_y_ref[...], halo[8:16]], axis=0)
 
     tail_t = tail.T
-    a = iota((256, 48), 0)
-    b = iota((256, 48), 1)
-    src, s = a >> 2, a & 3
-    a_n = 2 * ((src >> 3) & 3) + (src >> 5)
-    q = src & 7
-    p = b & 15
-    group = b >> 4
-    from_n = jnp.where(group == 0, n, jnp.where(group == 1, n + 7, n + 1)) & 7
-    right = (s == 0) & (a_n == from_n)
-    trend = pick_right(tail_t[0:64], one_hot(right & (2 * q == p + 1))) + pick_right(
-        tail_t[64:128], one_hot(right & (2 * q + 1 == p + 1))
-    )
+    trend = pick_right(tail_t[0:64], trend_pick[0]) + pick_right(tail_t[64:128], trend_pick[1])
     trend = jnp.concatenate([trend[56:64, 16:32], trend[:, 0:16], trend[0:8, 32:48]], axis=0)
 
-    j = iota((128, 128), 0)
-    col = iota((128, 128), 1)
-    src, jj = col & 63, col >> 6
-    order = one_hot(j == 16 * (2 * ((src >> 3) & 3) + (src >> 5)) + 4 * (src & 3) + 2 * ((src >> 2) & 1) + jj)
-    lift = tuple(mm(half, order).astype(BF16) for half in split2(phi_ext))
+    lift = tuple(mm(half, order_ref[...]).astype(BF16) for half in split2(phi_ext))
     modes = [
         jnp.concatenate([all_ref[pl.ds(2 * plane + jj, 64, stride=PARCEL), :] for jj in range(2)], axis=0)
         for plane in range(PLANES)
@@ -361,7 +364,7 @@
                 residual[at] = diag[at] * second
 
 
-def call(kernel, n_in, out_shapes, scratch=(), mebibytes=8):
+def call(kernel, n_in, out_shapes, scratch=(), mebibytes=8, cost=None):
     near = pl.BlockSpec(memory_space=pltpu.VMEM)
     return pl.pallas_call(
         kernel,
@@ -369,6 +372,7 @@
         out_specs=[near] * len(out_shapes) if isinstance(out_shapes, list) else near,
         out_shape=out_shapes,
         scratch_shapes=scratch,
+        cost_estimate=cost,
         compiler_params=pltpu.CompilerParams(vmem_limit_bytes=mebibytes * 1024 * 1024),
     )
 
@@ -378,9 +382,14 @@
 
 
 def local(coefficients, phi_x, phi_y, phi_z, log_trend):
-    packed = call(pack_kernel, 2, array(64 * SENT, 128))(coefficients, log_trend).reshape(64 * SENT, 1, 128)
+    shapes = [(256, 128), (128, 64 * SENT), (256, 64 * SENT), (256, 64 * SENT), (32, 64)]
+    shapes += [(128, 128), (16, 256), (2, 256, 48)]
+    cost = pl.CostEstimate(flops=1000000000, bytes_accessed=1000000, transcendentals=0)
+    chosen = call(choices_kernel, 0, [jax.ShapeDtypeStruct(shape, BF16) for shape in shapes], cost=cost)()
+    packed = call(pack_kernel, 3, array(64 * SENT, 128))(chosen[4], coefficients, log_trend)
+    packed = packed.reshape(64 * SENT, 1, 128)
     got = lax.all_to_all(packed, ("y", "h", "l"), 0, 0, tiled=True).reshape(64 * SENT, 128)
-    parcels = call(planes_kernel, 3, array(32 * PARCEL, 128))(got, phi_z, phi_y)
+    parcels = call(planes_kernel, 8, array(32 * PARCEL, 128))(got, phi_z, phi_y, *chosen[:5])
     parcels = parcels.reshape(32 * PARCEL, 1, 128)
     parcels = lax.all_to_all(parcels, ("x", "l", "y"), 0, 0, tiled=True)
     parcels = lax.all_gather(parcels.reshape(32 * PARCEL, 128), "c", tiled=True)
@@ -388,11 +397,11 @@
     field = pltpu.VMEM((PLANES, ROWS, NX), F32)
     *basis, diagonal, gram = call(
         solve_kernel,
-        3,
+        6,
         [own] * 6 + [array(32, 1, 128)],
         [field] * 9 + [pltpu.VMEM((2, PLANES * ROWS, 128), BF16)],
         32,
-    )(parcels, phi_y, phi_x)
+    )(parcels, phi_y, phi_x, *chosen[5:])
     gram = lax.all_to_all(gram, ("y", "x", "c"), 0, 0, tiled=True)
     gram = call(relay_kernel, 1, array(16, 1, 128))(gram)
     gram = lax.all_to_all(gram, ("h", "l"), 0, 0, tiled=True)

time: 90.4 us -> 90.1 us (level)
    pallas_call x3 -> x4, Pallas kernels: 5.35 us -> 5.78 us  [the longest x1 4.8 us: local(): call(solve_kernel, 6, [own] * 6 + [array(32, 1, 128)], [field] * 9 + [plt...]
where the time goes in v6:
time: 90.1 us; the launch traced here: 89.8 us
  blocking collectives  81.4 us (90%)
  Pallas kernels  6.95 us (8%)
    all_to_all x1, blocking collectives, local(): lax.all_to_all(packed, ('y', 'h', 'l'), 0, 0, tiled=True)  34.3 us
    all_to_all x1, blocking collectives, local(): parcels = lax.all_to_all(parcels, ('x', 'l', 'y'), 0, 0, tiled=True)  17.2 us
    all_to_all x1, blocking collectives, local(): gram = lax.all_to_all(gram, ('h', 'l'), 0, 0, tiled=True)  14.2 us
    all_to_all x1, blocking collectives, local(): gram = lax.all_to_all(gram, ('y', 'x', 'c'), 0, 0, tiled=True)  10.6 us
    all_gather x1, blocking collectives, local(): parcels = lax.all_gather(parcels.reshape(32 * PARCEL, 128), 'c', tiled=True)  5.24 us
    pallas_call x1, Pallas kernels, local(): call(solve_kernel, 6, [own] * 6 + [array(32, 1, 128)], [field] * 9 + [plt...  4.8 us

profile of v6, /device:TPU:1, one launch (start us, length us, event | category | flops | bytes accessed | tf_op | source)
XLA Modules:
  0.0 89.8 jit_solution(6723205404669082256)
XLA Ops:
  0.6 0.0 copy-start.3
  0.6 0.2 shard_map.68
  0.8 0.0 copy-start.4
  0.8 0.5 copy-done.3
  1.3 0.2 copy-done.4
  1.5 0.1 shard_map.69
  1.6 0.0 copy-start.1
  1.6 0.0 copy-start.2
  1.6 34.3 %all_to_all.20 = f32[320,1,128]{2,1,0:T(1,128)S(1)} all-to-all(f32[320,1,128]{2,1,0:T(1,128)S(1)} %bitcast.12), channel_id=1, replica_groups=mesh['y'=4,'h'=8,'l'=2,'x'=4,'c'=2] {'y','h','l'}, dimensions={0} | all-to-all | bytes 327680 | tf_op jit(solution)/shard_map/all_to_all | solution.py:391
  35.9 0.0 copy-done.1
  35.9 0.0 copy-done.2
  35.9 0.7 shard_map.70
  36.7 17.2 %all_to_all.21 = f32[896,1,128]{2,1,0:T(1,128)S(1)} all-to-all(f32[896,1,128]{2,1,0:T(1,128)S(1)} %bitcast.10), channel_id=1, replica_groups=mesh['y'=4,'h'=8,'l'=2,'x'=4,'c'=2] {'x','l','y'}, dimensions={0} | all-to-all | bytes 917504 | tf_op jit(solution)/shard_map/all_to_all | solution.py:394
  53.8 0.0 copy-start
  53.8 5.2 %all-gather = f32[1792,1,128]{2,0,1:T(8,128)S(1)} all-gather(f32[896,1,128]{2,0,1:T(8,128)S(1)} %bitcast.13), channel_id=2, replica_groups=mesh['y'=4,'h'=8,'l'=2,'x'=4,'c'=2] {'c'}, dimensions={0}, use_global_device_ids=true | all-gather | bytes 1376256 | tf_op jit(solution)/shard_map/all_gather | solution.py:395
  59.1 0.0 copy-done
  59.1 4.8 %shard_map.71 = (f32[2,64,512]{2,1,0:T(8,128)S(1)}, f32[2,64,512]{2,1,0:T(8,128)S(1)}, f32[2,64,512]{2,1,0:T(8,128)S(1)}, f32[2,64,512]{2,1,0:T(8,128)S(1)}, f32...) custom-call(f32[1792,128]{1,0:T(8,128)S(1)} %bitcast.9, f32[64,128]{1,0:T(8,128)S(1)} %copy-done.1, ...), custom_call_target="tpu_custom_call" | custom-call | tf_op jit(solution)/shard_map/pallas_call | solution.py:398
  63.9 10.6 %all_to_all.22.got_ref = f32[32,1,128]{2,1,0:T(1,128)S(1)} all-to-all(f32[32,1,128]{2,1,0:T(1,128)S(1)} %get-tuple-element.25), channel_id=1, replica_groups=mesh['y'=4,'h'=8,'l'=2,'x'=4,'c'=2] {'y','x','c'}, dimensions={0} | all-to-all | bytes 32768 | tf_op jit(solution)/shard_map/all_to_all | solution.py:405
  74.5 14.2 %all_to_all.23.got_ref = f32[16,1,128]{2,1,0:T(1,128)S(1)} all-to-all(f32[16,1,128]{2,1,0:T(1,128)S(1)} %shard_map.72), channel_id=1, replica_groups=mesh['y'=4,'h'=8,'l'=2,'x'=4,'c'=2] {'h','l'}, dimensions={0} | all-to-all | bytes 16384 | tf_op jit(solution)/shard_map/all_to_all | solution.py:407
  88.6 1.1 %shard_map.73 = (f32[2,64,512]{2,1,0:T(8,128)}, f32[2,64,512]{2,1,0:T(8,128)}) custom-call(f32[16,1,128]{2,1,0:T(1,128)S(1)} %all_to_all.23.got_ref, f32[2,64,512]{2,1,0:T(8,128)S(1)} %get-tuple-element.26.t0, f32[2,64,512]{2,1,0:T(8,128)S(1)} %get-tuple-element.27.t1, f32[2,64,512]{2,1,0:T(8,128)S(1)} %get-tuple-element.28.t2, ...), custom_call_target="tpu_custom_call" | custom-call | tf_op jit(solution)/shard_map/pallas_call | solution.py:408
  (1 shorter events, 0.0 us)
Async XLA Ops:
  0.6 0.7 copy-start.3
  0.8 0.7 copy-start.4
  1.6 34.3 %copy-start.1 = (f32[64,128]{1,0:T(8,128)S(1)}, f32[64,128]{1,0:T(8,128)}, u32[]{:S(2)}) copy-start(f32[64,128]{1,0:T(8,128)} %phi_y_ref.3) | copy-start | bytes 98308
  1.6 34.3 %copy-start.2 = (f32[128,128]{1,0:T(8,128)S(1)}, f32[128,128]{1,0:T(8,128)}, u32[]{:S(2)}) copy-start(f32[128,128]{1,0:T(8,128)} %phi_z_ref.1) | copy-start | bytes 196612
  53.8 5.2 %copy-start = (f32[512,128]{1,0:T(8,128)S(1)}, f32[512,128]{1,0:T(8,128)}, u32[]{:S(2)}) copy-start(f32[512,128]{1,0:T(8,128)} %phi_x_ref.1) | copy-start | bytes 786436

commit v7 on v6

--- a/solution.py
+++ b/solution.py
@@ -44,10 +44,6 @@
     return sum(mm(chosen, part) for part in split3(a))
 
 
-def pick_right(a, chosen):
-    return sum(mm(part, chosen) for part in split3(a))
-
-
 def dot3(a, b):
     (ah, al), (bh, bl) = a, b
     return mm(ah, bh) + (mm(al, bh) + mm(ah, bl))
@@ -57,56 +53,12 @@
     return jnp.where(condition, 1.0, 0.0).astype(BF16)
 
 
-def choices_kernel(modes, spread, keep, trends, edge_pick, order, halo_pick, trend_pick):
-    y, h, l = lax.axis_index("y"), lax.axis_index("h"), lax.axis_index("l")
-    n = 2 * lax.axis_index("x") + lax.axis_index("c")
-    mine = 4 * l + y
-
-    s1 = iota((32, 128), 0)
-    k1 = iota((32, 128), 1)
-    s5 = iota((32, 64 * SENT), 0)
-    row = iota((32, 64 * SENT), 1)
-    source = (row * 13108) >> 16
-    part = row - SENT * source
-    same_mode = one_hot((part < 4) & ((part & 1) == (s5 & 1)) & (s5 < 24))
-    trend_row = (part == 4) & (s5 == 24)
-    for to in range(8):
-        at = slice(32 * to, 32 * to + 32)
-        wide = 16 * (to & 3) + 2 * h + (to >> 2)
-        plane = (2 * wide - DEPTH + (s1 >> 1)) & 127
-        modes[at, :] = one_hot((plane == k1) & (s1 < 24))
-        keep[at, :] = same_mode
-        trends[at, :] = one_hot(trend_row & (source == ((wide - 3 + mine) & 63)))
-    k2 = iota((128, 64 * SENT), 0)
-    r2 = iota((128, 64 * SENT), 1)
-    source = (r2 * 13108) >> 16
-    part = r2 - SENT * source
-    spread[...] = one_hot((k2 == 2 * source + (part >> 1)) & (part < 4))
-    s6 = iota((32, 64), 0)
-    e6 = iota((32, 64), 1)
-    edge = 2 * mine + s6 - 25
-    edge = jnp.where(edge < 8, edge, edge + 48)
-    edge_pick[...] = one_hot((s6 >= 25) & (s6 < 27) & (e6 == edge))
-
-    row = iota((16, 256), 0)
-    col = iota((16, 256), 1)
-    edge = jnp.where(row < 8, row + 8, row - 8)
-    other = jnp.where(row < 8, n + 7, n + 1) & 7
-    halo_pick[...] = one_hot(col == ((other & 1) * 32 + (other >> 1) * 8 + (edge >> 1)) * 4 + 1 + (edge & 1))
-    a = iota((256, 48), 0)
-    b = iota((256, 48), 1)
-    src, s = a >> 2, a & 3
-    a_n = 2 * ((src >> 3) & 3) + (src >> 5)
-    p = b & 15
-    group = b >> 4
-    from_n = jnp.where(group == 0, n, jnp.where(group == 1, n + 7, n + 1)) & 7
-    right = (s == 0) & (a_n == from_n)
-    for r in range(2):
-        trend_pick[r] = one_hot(right & (2 * (src & 7) + r == p + 1))
+def choices_kernel(order, turn):
     j = iota((128, 128), 0)
     col = iota((128, 128), 1)
     src, jj = col & 63, col >> 6
     order[...] = one_hot(j == 16 * (2 * ((src >> 3) & 3) + (src >> 5)) + 4 * (src & 3) + 2 * ((src >> 2) & 1) + jj)
+    turn[...] = one_hot(j == 2 * src + jj)
 
 
 def pack_kernel(after_ref, coef_ref, trend_ref, out_ref):
@@ -122,15 +74,31 @@
             out_ref[start : start + 8 * SENT, :] = block
 
 
-def planes_kernel(got_ref, phi_z_ref, phi_y_ref, modes, spread, keep, trends, edge_pick, out_ref):
-    phi = split2(pick_left(modes[...], phi_z_ref[...]))
-    kept = keep[...].astype(F32)
-    high = (mm(phi[0], spread[...]) * kept).astype(BF16) + trends[...]
-    low = (mm(phi[1], spread[...]) * kept).astype(BF16)
-    result = dot3((high, low), split2(got_ref[...]))
-    edge_rows = pick_left(edge_pick[...], phi_y_ref[...])
-    for to in range(8):
-        block = (result[to * 32 : to * 32 + 32] + edge_rows)[0:PARCEL]
+def planes_kernel(got_ref, phi_z_ref, phi_y_ref, turn_ref, out_ref, block_ref):
+    y, h, l = lax.axis_index("y"), lax.axis_index("h"), lax.axis_index("l")
+    mine = 4 * l + y
+    p = iota((16, 128), 0)
+    k = iota((16, 128), 1)
+    wides = [16 * (to & 3) + 2 * h + (to >> 2) for to in range(8)]
+    modes = jnp.concatenate([one_hot(((2 * wide - DEPTH + p) & 127) == k) for wide in wides], axis=0)
+    phi = split2(pick_left(modes, phi_z_ref[...]))
+    phi = tuple(mm(half, turn_ref[...]).astype(BF16) for half in phi)
+    got = [
+        jnp.concatenate([got_ref[pl.ds(2 * r + jj, 64, stride=SENT), :] for r in range(2)], axis=0)
+        for jj in range(2)
+    ]
+    result = dot3(phi, split2(jnp.concatenate(got, axis=1)))
+    edge = 2 * mine + jnp.where(mine < 4, 0, 48)
+    for to, wide in enumerate(wides):
+        start = 32 * to
+        for jj in range(2):
+            rows = result[16 * to : 16 * to + PLANES, 128 * jj : 128 * jj + 128]
+            block_ref[pl.ds(start + jj, PLANES, stride=2), :] = rows
+        block_ref[start + 24 : start + 25, :] = got_ref[pl.ds(SENT * ((wide - 3 + mine) & 63) + 4, 1), :]
+        block_ref[start + 25 : start + 26, :] = phi_y_ref[pl.ds(edge, 1), :]
+        block_ref[start + 26 : start + 27, :] = phi_y_ref[pl.ds(edge + 1, 1), :]
+        block_ref[start + 27 : start + 28, :] = jnp.zeros((1, 128), F32)
+        block = block_ref[start : start + PARCEL, :]
         for x in range(4):
             at = (x * 8 + to) * PARCEL
             out_ref[at : at + PARCEL, :] = block
@@ -141,23 +109,29 @@
 
 
 def solve_kernel(
-    all_ref, phi_y_ref, phi_x_ref, order_ref, halo_pick, trend_pick,
+    all_ref, phi_y_ref, phi_x_ref, order_ref,
     t0_out, t1_out, t2_out, t3_out, t4_out, diag_out, gram_out,
     rec, fx, fy, fz, dinv, t0, t1, t2, t3, row_modes,
 ):
-    lower = iota((8, 128), 0) < 4
-
-    def tile(pair, at):
-        start = 2 * PARCEL * pair + 8 * at
-        return all_ref[start : start + 8, :]
-
-    tail = jnp.concatenate([jnp.where(lower, tile(pair, 3), tile(pair, 6)) for pair in range(32)], axis=0)
-    halo = pick_left(halo_pick[...], tail)
-    phi_ext = jnp.concatenate([halo[0:8], phi_y_ref[...], halo[8:16]], axis=0)
-
-    tail_t = tail.T
-    trend = pick_right(tail_t[0:64], trend_pick[0]) + pick_right(tail_t[64:128], trend_pick[1])
-    trend = jnp.concatenate([trend[56:64, 16:32], trend[:, 0:16], trend[0:8, 32:48]], axis=0)
+    n = 2 * lax.axis_index("x") + lax.axis_index("c")
+
+    def sent(other, index, s):
+        start = PARCEL * ((other & 1) * 32 + (other >> 1) * 8 + index) + s
+        return all_ref[pl.ds(start, 1), :]
+
+    before, after = (n + 7) & 7, (n + 1) & 7
+    low = [sent(before, e >> 1, 25 + (e & 1)) for e in range(8, 16)]
+    high = [sent(after, e >> 1, 25 + (e & 1)) for e in range(8)]
+    phi_ext = jnp.concatenate([*low, phi_y_ref[...], *high], axis=0)
+    trends = [sent(other, q, 24) for other in (n, before, after) for q in range(8)]
+    trends = jnp.concatenate([*trends, jnp.zeros((104, 128), F32)], axis=0).T
+
+    def trend(plane):
+        q, r = (plane + 1) >> 1, 64 * ((plane + 1) & 1)
+        return jnp.concatenate(
+            [trends[r + 56 : r + 64, 8 + q : 9 + q], trends[r : r + 64, q : q + 1], trends[r : r + 8, 16 + q : 17 + q]],
+            axis=0,
+        )
 
     lift = tuple(mm(half, order_ref[...]).astype(BF16) for half in split2(phi_ext))
     modes = [
@@ -176,7 +150,7 @@
         high, low = row_modes[0, at, :], row_modes[1, at, :]
         log_field = mm(jnp.concatenate([high, low, high], axis=1), all_x)
         for k in range(3):
-            rec[plane + k] = jnp.exp(-(log_field[k * ROWS : k * ROWS + ROWS] + trend[:, plane + k : plane + k + 1]))
+            rec[plane + k] = jnp.exp(-(log_field[k * ROWS : k * ROWS + ROWS] + trend(plane + k)))
 
     blocks = ROWS // 8
     sub = iota((8, NX), 0)
@@ -382,14 +356,14 @@
 
 
 def local(coefficients, phi_x, phi_y, phi_z, log_trend):
-    shapes = [(256, 128), (128, 64 * SENT), (256, 64 * SENT), (256, 64 * SENT), (32, 64)]
-    shapes += [(128, 128), (16, 256), (2, 256, 48)]
     cost = pl.CostEstimate(flops=1000000000, bytes_accessed=1000000, transcendentals=0)
-    chosen = call(choices_kernel, 0, [jax.ShapeDtypeStruct(shape, BF16) for shape in shapes], cost=cost)()
-    packed = call(pack_kernel, 3, array(64 * SENT, 128))(chosen[4], coefficients, log_trend)
+    order, turn = call(choices_kernel, 0, [jax.ShapeDtypeStruct((128, 128), BF16)] * 2, cost=cost)()
+    packed = call(pack_kernel, 3, array(64 * SENT, 128))(order, coefficients, log_trend)
     packed = packed.reshape(64 * SENT, 1, 128)
     got = lax.all_to_all(packed, ("y", "h", "l"), 0, 0, tiled=True).reshape(64 * SENT, 128)
-    parcels = call(planes_kernel, 8, array(32 * PARCEL, 128))(got, phi_z, phi_y, *chosen[:5])
+    parcels = call(planes_kernel, 4, array(32 * PARCEL, 128), [pltpu.VMEM((256, 128), F32)])(
+        got, phi_z, phi_y, turn
+    )
     parcels = parcels.reshape(32 * PARCEL, 1, 128)
     parcels = lax.all_to_all(parcels, ("x", "l", "y"), 0, 0, tiled=True)
     parcels = lax.all_gather(parcels.reshape(32 * PARCEL, 128), "c", tiled=True)
@@ -397,11 +371,11 @@
     field = pltpu.VMEM((PLANES, ROWS, NX), F32)
     *basis, diagonal, gram = call(
         solve_kernel,
-        6,
+        4,
         [own] * 6 + [array(32, 1, 128)],
         [field] * 9 + [pltpu.VMEM((2, PLANES * ROWS, 128), BF16)],
         32,
-    )(parcels, phi_y, phi_x, *chosen[5:])
+    )(parcels, phi_y, phi_x, order)
     gram = lax.all_to_all(gram, ("y", "x", "c"), 0, 0, tiled=True)
     gram = call(relay_kernel, 1, array(16, 1, 128))(gram)
     gram = lax.all_to_all(gram, ("h", "l"), 0, 0, tiled=True)

time: 90.1 us -> 89.3 us (level)
  no operation moved by 1% of the time
where the time goes in v7:
time: 89.3 us; the launch traced here: 89 us
  blocking collectives  81.4 us (91%)
  Pallas kernels  6.14 us (7%)
    all_to_all x1, blocking collectives, local(): lax.all_to_all(packed, ('y', 'h', 'l'), 0, 0, tiled=True)  34.3 us
    all_to_all x1, blocking collectives, local(): parcels = lax.all_to_all(parcels, ('x', 'l', 'y'), 0, 0, tiled=True)  17.2 us
    all_to_all x1, blocking collectives, local(): gram = lax.all_to_all(gram, ('h', 'l'), 0, 0, tiled=True)  14.2 us
    all_to_all x1, blocking collectives, local(): gram = lax.all_to_all(gram, ('y', 'x', 'c'), 0, 0, tiled=True)  10.6 us
    all_gather x1, blocking collectives, local(): parcels = lax.all_gather(parcels.reshape(32 * PARCEL, 128), 'c', tiled=True)  5.23 us
    pallas_call x1, Pallas kernels, local(): call(solve_kernel, 4, [own] * 6 + [array(32, 1, 128)], [field] * 9 + [plt...  4.33 us

profile of v7, /device:TPU:1, one launch (start us, length us, event | category | flops | bytes accessed | tf_op | source)
XLA Modules:
  0.0 89.0 jit_solution(3795672089860955055)
XLA Ops:
  0.6 0.0 copy-start.3
  0.7 0.0 copy-start.4
  0.7 0.7 copy-done.3
  1.3 0.0 copy-done.4
  1.4 0.1 shard_map.69
  1.4 0.0 copy-start.1
  1.5 0.0 copy-start.2
  1.5 34.3 %all_to_all.20 = f32[320,1,128]{2,1,0:T(1,128)S(1)} all-to-all(f32[320,1,128]{2,1,0:T(1,128)S(1)} %bitcast.11), channel_id=1, replica_groups=mesh['y'=4,'h'=8,'l'=2,'x'=4,'c'=2] {'y','h','l'}, dimensions={0} | all-to-all | bytes 327680 | tf_op jit(solution)/shard_map/all_to_all | solution.py:363
  35.8 0.0 copy-done.1
  35.8 0.0 copy-done.2
  35.8 0.5 shard_map.70
  36.3 17.2 %all_to_all.21 = f32[896,1,128]{2,1,0:T(1,128)S(1)} all-to-all(f32[896,1,128]{2,1,0:T(1,128)S(1)} %bitcast.10), channel_id=1, replica_groups=mesh['y'=4,'h'=8,'l'=2,'x'=4,'c'=2] {'x','l','y'}, dimensions={0} | all-to-all | bytes 917504 | tf_op jit(solution)/shard_map/all_to_all | solution.py:368
  53.5 0.0 copy-start
  53.5 5.2 %all-gather = f32[1792,1,128]{2,0,1:T(8,128)S(1)} all-gather(f32[896,1,128]{2,0,1:T(8,128)S(1)} %bitcast.13), channel_id=2, replica_groups=mesh['y'=4,'h'=8,'l'=2,'x'=4,'c'=2] {'c'}, dimensions={0}, use_global_device_ids=true | all-gather | bytes 1376256 | tf_op jit(solution)/shard_map/all_gather | solution.py:369
  58.7 0.0 copy-done
  58.7 4.3 %shard_map.71 = (f32[2,64,512]{2,1,0:T(8,128)S(1)}, f32[2,64,512]{2,1,0:T(8,128)S(1)}, f32[2,64,512]{2,1,0:T(8,128)S(1)}, f32[2,64,512]{2,1,0:T(8,128)S(1)}, f32...) custom-call(f32[1792,128]{1,0:T(8,128)S(1)} %bitcast.9, f32[64,128]{1,0:T(8,128)S(1)} %copy-done.1, ...), custom_call_target="tpu_custom_call" | custom-call | tf_op jit(solution)/shard_map/pallas_call | solution.py:372
  63.0 10.6 %all_to_all.22.got_ref = f32[32,1,128]{2,1,0:T(1,128)S(1)} all-to-all(f32[32,1,128]{2,1,0:T(1,128)S(1)} %get-tuple-element.13), channel_id=1, replica_groups=mesh['y'=4,'h'=8,'l'=2,'x'=4,'c'=2] {'y','x','c'}, dimensions={0} | all-to-all | bytes 32768 | tf_op jit(solution)/shard_map/all_to_all | solution.py:379
  73.7 14.2 %all_to_all.23.got_ref = f32[16,1,128]{2,1,0:T(1,128)S(1)} all-to-all(f32[16,1,128]{2,1,0:T(1,128)S(1)} %shard_map.72), channel_id=1, replica_groups=mesh['y'=4,'h'=8,'l'=2,'x'=4,'c'=2] {'h','l'}, dimensions={0} | all-to-all | bytes 16384 | tf_op jit(solution)/shard_map/all_to_all | solution.py:381
  87.8 1.1 %shard_map.73 = (f32[2,64,512]{2,1,0:T(8,128)}, f32[2,64,512]{2,1,0:T(8,128)}) custom-call(f32[16,1,128]{2,1,0:T(1,128)S(1)} %all_to_all.23.got_ref, f32[2,64,512]{2,1,0:T(8,128)S(1)} %get-tuple-element.14.t0, f32[2,64,512]{2,1,0:T(8,128)S(1)} %get-tuple-element.15.t1, f32[2,64,512]{2,1,0:T(8,128)S(1)} %get-tuple-element.16.t2, ...), custom_call_target="tpu_custom_call" | custom-call | tf_op jit(solution)/shard_map/pallas_call | solution.py:382
  (2 shorter events, 0.1 us)
Async XLA Ops:
  0.6 0.7 copy-start.3
  0.7 0.7 copy-start.4
  1.4 34.3 %copy-start.1 = (f32[64,128]{1,0:T(8,128)S(1)}, f32[64,128]{1,0:T(8,128)}, u32[]{:S(2)}) copy-start(f32[64,128]{1,0:T(8,128)} %phi_y_ref.3) | copy-start | bytes 98308
  1.5 34.3 %copy-start.2 = (f32[128,128]{1,0:T(8,128)S(1)}, f32[128,128]{1,0:T(8,128)}, u32[]{:S(2)}) copy-start(f32[128,128]{1,0:T(8,128)} %phi_z_ref.1) | copy-start | bytes 196612
  53.5 5.2 %copy-start = (f32[512,128]{1,0:T(8,128)S(1)}, f32[512,128]{1,0:T(8,128)}, u32[]{:S(2)}) copy-start(f32[512,128]{1,0:T(8,128)} %phi_x_ref.1) | copy-start | bytes 786436

commit v8 on v7

--- a/solution.py
+++ b/solution.py
@@ -376,9 +376,9 @@
         [field] * 9 + [pltpu.VMEM((2, PLANES * ROWS, 128), BF16)],
         32,
     )(parcels, phi_y, phi_x, order)
-    gram = lax.all_to_all(gram, ("y", "x", "c"), 0, 0, tiled=True)
+    gram = lax.all_to_all(gram, ("c", "h", "l"), 0, 0, tiled=True)
     gram = call(relay_kernel, 1, array(16, 1, 128))(gram)
-    gram = lax.all_to_all(gram, ("h", "l"), 0, 0, tiled=True)
+    gram = lax.all_to_all(gram, ("y", "x"), 0, 0, tiled=True)
     return tuple(call(combine_kernel, 7, [own, own])(gram, *basis, diagonal))
 
 

time: 89.3 us -> 89.4 us (level)
  no operation moved by 1% of the time
where the time goes in v8:
time: 89.4 us; the launch traced here: 89.1 us
  blocking collectives  81.6 us (91%)
  Pallas kernels  6.14 us (7%)
    all_to_all x1, blocking collectives, local(): lax.all_to_all(packed, ('y', 'h', 'l'), 0, 0, tiled=True)  34.3 us
    all_to_all x1, blocking collectives, local(): parcels = lax.all_to_all(parcels, ('x', 'l', 'y'), 0, 0, tiled=True)  17.2 us
    all_to_all x1, blocking collectives, local(): gram = lax.all_to_all(gram, ('c', 'h', 'l'), 0, 0, tiled=True)  15.5 us
    all_to_all x1, blocking collectives, local(): gram = lax.all_to_all(gram, ('y', 'x'), 0, 0, tiled=True)  9.37 us
    all_gather x1, blocking collectives, local(): parcels = lax.all_gather(parcels.reshape(32 * PARCEL, 128), 'c', tiled=True)  5.23 us
    pallas_call x1, Pallas kernels, local(): call(solve_kernel, 4, [own] * 6 + [array(32, 1, 128)], [field] * 9 + [plt...  4.33 us

profile of v8, /device:TPU:1, one launch (start us, length us, event | category | flops | bytes accessed | tf_op | source)
XLA Modules:
  0.0 89.1 jit_solution(5728989222230454552)
XLA Ops:
  0.6 0.0 copy-start.3
  0.7 0.0 copy-start.4
  0.7 0.7 copy-done.3
  1.3 0.0 copy-done.4
  1.4 0.1 shard_map.69
  1.4 0.0 copy-start.1
  1.5 0.0 copy-start.2
  1.5 34.3 %all_to_all.20 = f32[320,1,128]{2,1,0:T(1,128)S(1)} all-to-all(f32[320,1,128]{2,1,0:T(1,128)S(1)} %bitcast.11), channel_id=1, replica_groups=mesh['y'=4,'h'=8,'l'=2,'x'=4,'c'=2] {'y','h','l'}, dimensions={0} | all-to-all | bytes 327680 | tf_op jit(solution)/shard_map/all_to_all | solution.py:363
  35.8 0.0 copy-done.1
  35.8 0.0 copy-done.2
  35.8 0.5 shard_map.70
  36.3 17.2 %all_to_all.21 = f32[896,1,128]{2,1,0:T(1,128)S(1)} all-to-all(f32[896,1,128]{2,1,0:T(1,128)S(1)} %bitcast.10), channel_id=1, replica_groups=mesh['y'=4,'h'=8,'l'=2,'x'=4,'c'=2] {'x','l','y'}, dimensions={0} | all-to-all | bytes 917504 | tf_op jit(solution)/shard_map/all_to_all | solution.py:368
  53.5 0.0 copy-start
  53.5 5.2 %all-gather = f32[1792,1,128]{2,0,1:T(8,128)S(1)} all-gather(f32[896,1,128]{2,0,1:T(8,128)S(1)} %bitcast.13), channel_id=2, replica_groups=mesh['y'=4,'h'=8,'l'=2,'x'=4,'c'=2] {'c'}, dimensions={0}, use_global_device_ids=true | all-gather | bytes 1376256 | tf_op jit(solution)/shard_map/all_gather | solution.py:369
  58.7 0.0 copy-done
  58.7 4.3 %shard_map.71 = (f32[2,64,512]{2,1,0:T(8,128)S(1)}, f32[2,64,512]{2,1,0:T(8,128)S(1)}, f32[2,64,512]{2,1,0:T(8,128)S(1)}, f32[2,64,512]{2,1,0:T(8,128)S(1)}, f32...) custom-call(f32[1792,128]{1,0:T(8,128)S(1)} %bitcast.9, f32[64,128]{1,0:T(8,128)S(1)} %copy-done.1, ...), custom_call_target="tpu_custom_call" | custom-call | tf_op jit(solution)/shard_map/pallas_call | solution.py:372
  63.0 15.5 %all_to_all.22.got_ref = f32[32,1,128]{2,1,0:T(1,128)S(1)} all-to-all(f32[32,1,128]{2,1,0:T(1,128)S(1)} %get-tuple-element.13), channel_id=1, replica_groups=mesh['y'=4,'h'=8,'l'=2,'x'=4,'c'=2] {'c','h','l'}, dimensions={0} | all-to-all | bytes 32768 | tf_op jit(solution)/shard_map/all_to_all | solution.py:379
  78.6 9.4 %all_to_all.23.got_ref = f32[16,1,128]{2,1,0:T(1,128)S(1)} all-to-all(f32[16,1,128]{2,1,0:T(1,128)S(1)} %shard_map.72), channel_id=1, replica_groups=mesh['y'=4,'h'=8,'l'=2,'x'=4,'c'=2] {'y','x'}, dimensions={0} | all-to-all | bytes 16384 | tf_op jit(solution)/shard_map/all_to_all | solution.py:381
  88.0 1.1 %shard_map.73 = (f32[2,64,512]{2,1,0:T(8,128)}, f32[2,64,512]{2,1,0:T(8,128)}) custom-call(f32[16,1,128]{2,1,0:T(1,128)S(1)} %all_to_all.23.got_ref, f32[2,64,512]{2,1,0:T(8,128)S(1)} %get-tuple-element.14.t0, f32[2,64,512]{2,1,0:T(8,128)S(1)} %get-tuple-element.15.t1, f32[2,64,512]{2,1,0:T(8,128)S(1)} %get-tuple-element.16.t2, ...), custom_call_target="tpu_custom_call" | custom-call | tf_op jit(solution)/shard_map/pallas_call | solution.py:382
  (2 shorter events, 0.1 us)
Async XLA Ops:
  0.6 0.7 copy-start.3
  0.7 0.7 copy-start.4
  1.4 34.3 %copy-start.1 = (f32[64,128]{1,0:T(8,128)S(1)}, f32[64,128]{1,0:T(8,128)}, u32[]{:S(2)}) copy-start(f32[64,128]{1,0:T(8,128)} %phi_y_ref.3) | copy-start | bytes 98308
  1.5 34.3 %copy-start.2 = (f32[128,128]{1,0:T(8,128)S(1)}, f32[128,128]{1,0:T(8,128)}, u32[]{:S(2)}) copy-start(f32[128,128]{1,0:T(8,128)} %phi_z_ref.1) | copy-start | bytes 196612
  53.5 5.2 %copy-start = (f32[512,128]{1,0:T(8,128)S(1)}, f32[512,128]{1,0:T(8,128)}, u32[]{:S(2)}) copy-start(f32[512,128]{1,0:T(8,128)} %phi_x_ref.1) | copy-start | bytes 786436

commit v9 on v8

--- a/solution.py
+++ b/solution.py
@@ -15,7 +15,7 @@
 NX = 512
 SENT = 5
 PARCEL = 28
-GRAM = [(i, j) for i in range(ITERS + 1) for j in range(i, ITERS + 1) if i < ITERS]
+GRAM = [(0, j) for j in range(ITERS + 1)] + [(j, ITERS) for j in range(1, ITERS)]
 BF16 = jnp.bfloat16
 F32 = jnp.float32
 
@@ -241,9 +241,9 @@
             for ref, field in zip((t0_out, t1_out, t2_out, t3_out, t4_out), basis):
                 ref[index, to, :] = field
             diag_out[index, to, :] = 4.0 * diagonal
-            weighted = [diagonal * field for field in basis[:ITERS]]
+            weighted = {0: diagonal * basis[0], ITERS: diagonal * basis[ITERS]}
             for at_sum, (i, k) in enumerate(GRAM):
-                product = weighted[i] * basis[k]
+                product = weighted[i] * basis[k] if i == 0 else weighted[k] * basis[i]
                 product = (product[:, 0:128] + product[:, 128:256]) + (product[:, 256:384] + product[:, 384:512])
                 sums[at_sum] = sums[at_sum] + product
 
@@ -275,6 +275,12 @@
     for at_sum, (i, k) in enumerate(GRAM):
         value = jnp.sum(jnp.where(lane == at_sum, total, 0.0), axis=1, keepdims=True)
         gram[i, k] = gram[k, i] = jnp.broadcast_to(value, (8, 128))
+    moments = [gram[0, k] for k in range(ITERS + 1)]
+    for i in range(1, ITERS):
+        moments.append(gram[i, ITERS] - sum(moments[ITERS - i + 2 : ITERS + i : 2], moments[ITERS - i]))
+    for i in range(1, ITERS):
+        for k in range(i, ITERS):
+            gram[i, k] = gram[k, i] = sum(moments[k - i + 2 : k + i + 1 : 2], moments[k - i])
     zero = jnp.zeros((8, 128), F32)
 
     def shifted(a):

time: 89.4 us -> 89.3 us (level)
  no operation moved by 1% of the time
where the time goes in v9:
time: 89.3 us; the launch traced here: 88.9 us
  blocking collectives  81.6 us (91%)
  Pallas kernels  5.99 us (7%)
    all_to_all x1, blocking collectives, local(): lax.all_to_all(packed, ('y', 'h', 'l'), 0, 0, tiled=True)  34.3 us
    all_to_all x1, blocking collectives, local(): parcels = lax.all_to_all(parcels, ('x', 'l', 'y'), 0, 0, tiled=True)  17.2 us
    all_to_all x1, blocking collectives, local(): gram = lax.all_to_all(gram, ('c', 'h', 'l'), 0, 0, tiled=True)  15.5 us
    all_to_all x1, blocking collectives, local(): gram = lax.all_to_all(gram, ('y', 'x'), 0, 0, tiled=True)  9.37 us
    all_gather x1, blocking collectives, local(): parcels = lax.all_gather(parcels.reshape(32 * PARCEL, 128), 'c', tiled=True)  5.23 us
    pallas_call x1, Pallas kernels, local(): call(solve_kernel, 4, [own] * 6 + [array(32, 1, 128)], [field] * 9 + [plt...  4.19 us

profile of v9, /device:TPU:1, one launch (start us, length us, event | category | flops | bytes accessed | tf_op | source)
XLA Modules:
  0.0 88.9 jit_solution(8259677444995893795)
XLA Ops:
  0.6 0.0 copy-start.3
  0.7 0.0 copy-start.4
  0.7 0.7 copy-done.3
  1.3 0.0 copy-done.4
  1.4 0.1 shard_map.69
  1.4 0.0 copy-start.1
  1.5 0.0 copy-start.2
  1.5 34.3 %all_to_all.20 = f32[320,1,128]{2,1,0:T(1,128)S(1)} all-to-all(f32[320,1,128]{2,1,0:T(1,128)S(1)} %bitcast.11), channel_id=1, replica_groups=mesh['y'=4,'h'=8,'l'=2,'x'=4,'c'=2] {'y','h','l'}, dimensions={0} | all-to-all | bytes 327680 | tf_op jit(solution)/shard_map/all_to_all | solution.py:369
  35.8 0.0 copy-done.1
  35.8 0.0 copy-done.2
  35.8 0.5 shard_map.70
  36.3 17.2 %all_to_all.21 = f32[896,1,128]{2,1,0:T(1,128)S(1)} all-to-all(f32[896,1,128]{2,1,0:T(1,128)S(1)} %bitcast.10), channel_id=1, replica_groups=mesh['y'=4,'h'=8,'l'=2,'x'=4,'c'=2] {'x','l','y'}, dimensions={0} | all-to-all | bytes 917504 | tf_op jit(solution)/shard_map/all_to_all | solution.py:374
  53.5 0.0 copy-start
  53.5 5.2 %all-gather = f32[1792,1,128]{2,0,1:T(8,128)S(1)} all-gather(f32[896,1,128]{2,0,1:T(8,128)S(1)} %bitcast.13), channel_id=2, replica_groups=mesh['y'=4,'h'=8,'l'=2,'x'=4,'c'=2] {'c'}, dimensions={0}, use_global_device_ids=true | all-gather | bytes 1376256 | tf_op jit(solution)/shard_map/all_gather | solution.py:375
  58.7 0.0 copy-done
  58.7 4.2 %shard_map.71 = (f32[2,64,512]{2,1,0:T(8,128)S(1)}, f32[2,64,512]{2,1,0:T(8,128)S(1)}, f32[2,64,512]{2,1,0:T(8,128)S(1)}, f32[2,64,512]{2,1,0:T(8,128)S(1)}, f32...) custom-call(f32[1792,128]{1,0:T(8,128)S(1)} %bitcast.9, f32[64,128]{1,0:T(8,128)S(1)} %copy-done.1, ...), custom_call_target="tpu_custom_call" | custom-call | tf_op jit(solution)/shard_map/pallas_call | solution.py:378
  62.9 15.5 %all_to_all.22.got_ref = f32[32,1,128]{2,1,0:T(1,128)S(1)} all-to-all(f32[32,1,128]{2,1,0:T(1,128)S(1)} %get-tuple-element.13), channel_id=1, replica_groups=mesh['y'=4,'h'=8,'l'=2,'x'=4,'c'=2] {'c','h','l'}, dimensions={0} | all-to-all | bytes 32768 | tf_op jit(solution)/shard_map/all_to_all | solution.py:385
  78.4 9.4 %all_to_all.23.got_ref = f32[16,1,128]{2,1,0:T(1,128)S(1)} all-to-all(f32[16,1,128]{2,1,0:T(1,128)S(1)} %shard_map.72), channel_id=1, replica_groups=mesh['y'=4,'h'=8,'l'=2,'x'=4,'c'=2] {'y','x'}, dimensions={0} | all-to-all | bytes 16384 | tf_op jit(solution)/shard_map/all_to_all | solution.py:387
  87.8 1.1 %shard_map.73 = (f32[2,64,512]{2,1,0:T(8,128)}, f32[2,64,512]{2,1,0:T(8,128)}) custom-call(f32[16,1,128]{2,1,0:T(1,128)S(1)} %all_to_all.23.got_ref, f32[2,64,512]{2,1,0:T(8,128)S(1)} %get-tuple-element.14.t0, f32[2,64,512]{2,1,0:T(8,128)S(1)} %get-tuple-element.15.t1, f32[2,64,512]{2,1,0:T(8,128)S(1)} %get-tuple-element.16.t2, ...), custom_call_target="tpu_custom_call" | custom-call | tf_op jit(solution)/shard_map/pallas_call | solution.py:388
  (2 shorter events, 0.1 us)
Async XLA Ops:
  0.6 0.7 copy-start.3
  0.7 0.7 copy-start.4
  1.4 34.3 %copy-start.1 = (f32[64,128]{1,0:T(8,128)S(1)}, f32[64,128]{1,0:T(8,128)}, u32[]{:S(2)}) copy-start(f32[64,128]{1,0:T(8,128)} %phi_y_ref.3) | copy-start | bytes 98308
  1.5 34.3 %copy-start.2 = (f32[128,128]{1,0:T(8,128)S(1)}, f32[128,128]{1,0:T(8,128)}, u32[]{:S(2)}) copy-start(f32[128,128]{1,0:T(8,128)} %phi_z_ref.1) | copy-start | bytes 196612
  53.5 5.2 %copy-start = (f32[512,128]{1,0:T(8,128)S(1)}, f32[512,128]{1,0:T(8,128)}, u32[]{:S(2)}) copy-start(f32[512,128]{1,0:T(8,128)} %phi_x_ref.1) | copy-start | bytes 786436
